TPU v7x, 32 devices: a whole 2x2x4 slice. The times are simulated.
32 devices in a mesh: cfg: 2 (over x), section: 8 (over z, core), patch: 2 (over y).
Axes of the slice: x: 2, y: 2, z: 4, core: 2. Of those that a mesh axis runs over, the one named last changes fastest.
Arguments:
- latent: float32 [4, 16, 64], replicated, may hold values from -6 to 6
- w_in: bfloat16 [64, 2432], P(None, 'patch'), may hold values from -0.75 to 0.75
- modulation: float32 [8, 2, 3, 2432], P('section', 'cfg'), may hold values from -3 to 3
- w_qkv: bfloat16 [8, 3, 1536, 2432], P('section', None, 'patch'), may hold values from -0.125 to 0.125
- text_kv: bfloat16 [8, 2, 333, 24, 128], P('section', 'cfg', None, 'patch'), may hold values from -6 to 6
- stale_kv: bfloat16 [8, 2, 64, 24, 128], P('section', 'cfg', None, 'patch'), may hold values from -6 to 6
- w_out: bfloat16 [8, 1536, 2432], P('section', None, 'patch'), may hold values from -0.625 to 0.625
- w_final: bfloat16 [2432, 64], P('patch'), may hold values from -0.125 to 0.125
- guidance: float32 [1], replicated, may hold values from 3 to 7
- step_index: int32 [1], replicated, may hold values from 0 to 27
Outputs:
- next_latent: float32 [16, 256], P('patch', ('cfg', 'section'))
All inputs are finite; a program needn't handle non-finite values.
Results may differ from a plain program's by a relative error of at most 0.013.
Values may be sent and summed in bfloat16 or wider, within the bound.
A program may use at most 64 MiB of HBM per device.

v0:
```python
import jax
import jax.numpy as jnp
from jax import lax
from jax.sharding import PartitionSpec as P

HEAD_DIM = 64
STEPS = 28


SHIFT_SIGMA = 3.0
EPS_NORM = 1e-06


def from_behind(value, axis, steps):
    count = lax.axis_size(axis)
    leading, last = (max(0, -steps), min(count, count - steps))
    return lax.ppermute(value, axis, [(source, source + steps) for source in range(leading, last)])


def swapped(block, axis, bit):
    count = lax.axis_size(axis)
    route = []
    for low in range(count):
        high = low | 1 << bit
        if high != low and high < count:
            route += [(low, high), (high, low)]
    return lax.ppermute(block, axis, route)


def broadcast(value, axis, source):
    kept = jnp.where(lax.axis_index(axis) == source, value, 0).astype(value.dtype)
    return lax.psum(kept, axis)


def sigma_at(position):
    level = 1.0 - position.astype(jnp.float32) / STEPS
    return SHIFT_SIGMA * level / (1.0 + (SHIFT_SIGMA - 1.0) * level)


def rms_heads(values):
    shaped = values.astype(jnp.float32).reshape(values.shape[:-1] + (-1, HEAD_DIM))
    scaled = shaped * lax.rsqrt(jnp.mean(shaped * shaped, axis=-1, keepdims=True) + EPS_NORM)
    return scaled.astype(jnp.bfloat16)


def attend(queries, all_keys, all_values):
    scores = (
        jnp.einsum("rhd,khd->hrk", queries, all_keys, preferred_element_type=jnp.float32)
        / HEAD_DIM**0.5
    )
    weights_soft = jax.nn.softmax(scores, axis=-1).astype(jnp.bfloat16)
    attended = jnp.einsum(
        "hrk,khd->rhd", weights_soft, all_values, preferred_element_type=jnp.float32
    )
    return attended.astype(jnp.bfloat16).reshape(queries.shape[0], -1)


def widen(column_rows):
    return lax.all_gather(column_rows, "patch", axis=1, tiled=True)


def on_device(
    latent, w_in, modulation, w_qkv, text_kv, stale_kv, w_out, w_final, guidance, step_index
):
    sections = lax.axis_size("section")
    section_index = lax.axis_index("section")
    patch_count = lax.axis_size("patch")
    patch_index = lax.axis_index("patch")
    branch_index = lax.axis_index("cfg")
    micro_count = latent.shape[0]
    batch_rows = latent.shape[1]
    chan_count = latent.shape[2]
    own_rows = batch_rows // patch_count
    columns = w_in.shape[1]
    model_width = columns * patch_count
    local_inner = w_qkv.shape[2]
    local_heads = local_inner // HEAD_DIM
    shifts = modulation[0, 0]
    gate_cols = lax.dynamic_slice_in_dim(shifts[2], patch_index * columns, columns, 0)
    w_proj = w_qkv[0].reshape(3 * local_inner, model_width)
    text_pair = text_kv[0, 0]
    w_back = w_out[0]
    latent_bf = latent.astype(jnp.bfloat16)
    zero_index = jnp.zeros((), jnp.int32)

    def block_work(full_rows, buffer, micro_index):
        residual = full_rows.astype(jnp.float32)
        row_mean = jnp.mean(residual, axis=-1, keepdims=True)
        row_var = jnp.mean((residual - row_mean) ** 2, axis=-1, keepdims=True)
        normed = (residual - row_mean) * lax.rsqrt(row_var + EPS_NORM)
        normed = (normed * (1.0 + shifts[1]) + shifts[0]).astype(jnp.bfloat16)
        projected = lax.dot_general(
            normed, w_proj, (((1,), (1,)), ((), ())), preferred_element_type=jnp.float32
        )
        projected = projected.astype(jnp.bfloat16).reshape(batch_rows, 3, local_inner)
        new_pair = jnp.concatenate(
            [
                projected[:, 1].reshape(batch_rows, local_heads, HEAD_DIM),
                projected[:, 2].reshape(batch_rows, local_heads, HEAD_DIM),
            ],
            axis=-1,
        )
        buffer = lax.dynamic_update_slice(
            buffer, new_pair, (micro_index * batch_rows, zero_index, zero_index)
        )
        joined = jnp.concatenate([text_pair, buffer], axis=0)
        all_keys = rms_heads(joined[:, :, :HEAD_DIM].reshape(joined.shape[0], local_inner))
        all_values = joined[:, :, HEAD_DIM:]
        attended = attend(rms_heads(projected[:, 0]), all_keys, all_values)
        update_cols = jnp.dot(
            lax.all_gather(attended, "patch", axis=1, tiled=True),
            w_back,
            preferred_element_type=jnp.float32,
        )
        own_cols = lax.dynamic_slice_in_dim(full_rows, patch_index * columns, columns, 1)
        return (
            (own_cols.astype(jnp.float32) + gate_cols * update_cols).astype(jnp.bfloat16),
            buffer,
        )

    def velocity_of(new_cols):
        return lax.psum_scatter(
            jnp.dot(new_cols, w_final, preferred_element_type=jnp.float32),
            "patch",
            scatter_dimension=0,
            tiled=True,
        )

    def round_step(round_index, carry):
        incoming, buffer, velocity = carry
        micro_index = round_index - section_index
        active = (micro_index >= 0) & (micro_index < micro_count)
        clamped = jnp.clip(micro_index, 0, micro_count - 1)

        def working(operands):
            arrived, held, speeds = operands
            patch_latent = lax.dynamic_index_in_dim(latent_bf, clamped, 0, keepdims=False)
            embed_cols = jnp.dot(patch_latent, w_in, preferred_element_type=jnp.float32).astype(
                jnp.bfloat16
            )
            full_rows = widen(jnp.where(section_index == 0, embed_cols, arrived))
            new_cols, held = block_work(full_rows, held, clamped)
            speed = velocity_of(new_cols)
            speeds = jnp.where(
                section_index == sections - 1,
                lax.dynamic_update_index_in_dim(speeds, speed, clamped, 0),
                speeds,
            )
            return (new_cols, held, speeds)

        def waiting(operands):
            arrived, held, speeds = operands
            return (jnp.zeros_like(arrived), held, speeds)

        outgoing, buffer, velocity = lax.cond(
            active, working, waiting, (incoming, buffer, velocity)
        )
        incoming = from_behind(outgoing, "section", 1)
        return (incoming, buffer, velocity)

    start = (
        jnp.zeros((batch_rows, columns), jnp.bfloat16),
        stale_kv[0, 0],
        jnp.zeros((micro_count, own_rows, chan_count), jnp.float32),
    )
    unused_rows, unused_buffer, velocity = lax.fori_loop(
        0, micro_count + sections - 1, round_step, start
    )
    wide_count = micro_count * chan_count
    half_width = wide_count // 2
    flat_speed = jnp.transpose(velocity, (1, 0, 2)).reshape(own_rows, wide_count)
    kept_half = lax.dynamic_slice_in_dim(flat_speed, branch_index * half_width, half_width, 1)
    sent_half = lax.dynamic_slice_in_dim(flat_speed, (1 - branch_index) * half_width, half_width, 1)
    partner = swapped(sent_half, "cfg", 0)
    is_conditional = branch_index == 0
    conditional = jnp.where(is_conditional, kept_half, partner)
    unconditional = jnp.where(is_conditional, partner, kept_half)
    guided = unconditional + guidance[0] * (conditional - unconditional)
    step_size = sigma_at(step_index[0] + 1) - sigma_at(step_index[0])
    own_latent = lax.dynamic_slice_in_dim(latent, patch_index * own_rows, own_rows, 1)
    flat_latent = jnp.transpose(own_latent, (1, 0, 2)).reshape(own_rows, wide_count)
    latent_half = lax.dynamic_slice_in_dim(flat_latent, branch_index * half_width, half_width, 1)
    result = latent_half + step_size * guided
    shared = broadcast(result, "section", sections - 1)
    section_width = half_width // sections
    return lax.dynamic_slice_in_dim(shared, section_index * section_width, section_width, 1)


def solution(mesh):
    in_specs = (
        P(),
        P(None, "patch"),
        P("section", "cfg", None, None),
        P("section", None, "patch", None),
        P("section", "cfg", None, "patch", None),
        P("section", "cfg", None, "patch", None),
        P("section", None, "patch"),
        P("patch", None),
        P(),
        P(),
    )
    out_specs = P("patch", ("cfg", "section"))
    return jax.shard_map(
        on_device, mesh=mesh, in_specs=in_specs, out_specs=out_specs, check_vma=False
    )
```

profile of v0, /device:TPU:0, one launch (start us, length us, event | category | flops | bytes accessed | tf_op | source)
XLA Modules:
  0.0 438.9 jit_solution(15467874068345513296)
XLA Ops:
  4.7 6.1 %copy.62 = bf16[1,1536,1216]{2,1,0:T(8,128)(2,1)} copy(bf16[1,1536,1216]{1,2,0:T(8,128)(2,1)} %param.20) | data formatting | bytes 7471104 | tf_op args[6]
  10.9 314.7 %while.17 = (s32[]{:T(128)}, bf16[16,1216]{1,0:T(8,128)(2,1)S(1)}, bf16[64,12,128]{0,2,1:T(8,128)(2,1)S(1)}, f32[4,8,64]{2,1,0:T(8,128)S(1)}, s32[]{:T(128)}, /*...) while((s32[]{:T(128)}, bf16[16,1216]{1,0:T(8,128)(2,1)S(1)}, ...), condition=%wide.region_10.11_spmd, body=%wide.region_0.10_spmd.sunk | while | flops 269630784 | bytes 21897548 | solution.py:166
  11.0 33.3 %conditional.2 = (bf16[16,1216]{1,0:T(8,128)(2,1)}, bf16[64,12,128]{0,2,1:T(8,128)(2,1)S(1)}, f32[4,8,64]{2,1,0:T(8,128)S(1)}) conditional(s32[]{:T(128)} %convert_element_type.132, (bf16[64,12,128]{0,2,1:T(8,128)(2,1)S(1)}, f32[4,8,64]{2,1,0:T(8,128)S(1)}) %tuple.48, (s32[]{:T(128)}, s32[]{:T(128)}, bf16[4,16,64]{2,1,0:T(8,128)(2,1)S(1)}, ...), branch_computations={%region_1.1_spmd, %region_2.9_spmd} | conditional | flops 269630784 | bytes 21741536 | solution.py:155
  13.1 5.6 %all-gather = bf16[2,1216,16]{1,2,0:T(8,128)(2,1)S(1)} all-gather(bf16[1,1216,16]{1,2,0:T(8,128)(2,1)S(1)} %fusion.4), channel_id=1, replica_groups=mesh['cfg'=2,'section'=8,'patch'=2] {'patch'}, dimensions={0}, use_global_device_ids=true | all-gather | bytes 116736 | tf_op jit(solution)/shard_map/while/body/eval_jaxpr/cond/branch_1_fun/all_gather | solution.py:59
  19.3 7.2 %convolution_convert_fusion = bf16[16,2304]{1,0:T(8,128)(2,1)S(1)} fusion(bf16[2304,2432]{1,0:T(8,128)(2,1)} %get-tuple-element.270, bf16[2432,16]{0,1:T(8,128)(2,1)S(1)} %reshape.83, f32[16]{0:T(128)S(1)} %add_rsqrt_fusion.2, f32[16]{0:T(128)S(1)} %broadcast_multiply_fusion, f32[2432]{0:T(1024)S(1)} %get-tuple-element.365, f32[2432]{0:T(1024)S(1)} %get-tuple-element.364), kind=kOutput, calls=%fused_computation.1 | convolution fusion | flops 179576832 | bytes 11377792 | tf_op jit(solution)/shard_map/while/body/eval_jaxpr/cond/branch_1_fun/dot_general | solution.py:92
  30.4 4.5 %all_gather.5 = bf16[16,1536]{1,0:T(8,128)(2,1)S(1)} all-gather(bf16[16,768]{1,0:T(8,128)(2,1)S(1)} %reshape.65), channel_id=1, replica_groups=mesh['cfg'=2,'section'=8,'patch'=2] {'patch'}, dimensions={1}, use_global_device_ids=true | all-gather | bytes 73728 | tf_op jit(solution)/shard_map/while/body/eval_jaxpr/cond/branch_1_fun/all_gather | solution.py:111
  39.2 5.0 %all-reduce = f32[16,64]{1,0:T(8,128)S(1)} all-reduce(f32[16,64]{1,0:T(8,128)S(1)} %fusion.54), channel_id=2, replica_groups=mesh['cfg'=2,'section'=8,'patch'=2] {'patch'}, use_global_device_ids=true, to_apply=%region_9.8.clone | all-reduce | flops 1024 | bytes 8192 | tf_op jit(solution)/shard_map/while/body/eval_jaxpr/cond
  46.6 34.7 %conditional.2 = (bf16[16,1216]{1,0:T(8,128)(2,1)}, bf16[64,12,128]{0,2,1:T(8,128)(2,1)S(1)}, f32[4,8,64]{2,1,0:T(8,128)S(1)}) conditional(s32[]{:T(128)} %convert_element_type.132, (bf16[64,12,128]{0,2,1:T(8,128)(2,1)S(1)}, f32[4,8,64]{2,1,0:T(8,128)S(1)}) %tuple.48, (s32[]{:T(128)}, s32[]{:T(128)}, bf16[4,16,64]{2,1,0:T(8,128)(2,1)S(1)}, ...), branch_computations={%region_1.1_spmd, %region_2.9_spmd} | conditional | flops 269630784 | bytes 21741536 | solution.py:155
  48.7 4.8 %all-gather = bf16[2,1216,16]{1,2,0:T(8,128)(2,1)S(1)} all-gather(bf16[1,1216,16]{1,2,0:T(8,128)(2,1)S(1)} %fusion.4), channel_id=1, replica_groups=mesh['cfg'=2,'section'=8,'patch'=2] {'patch'}, dimensions={0}, use_global_device_ids=true | all-gather | bytes 116736 | tf_op jit(solution)/shard_map/while/body/eval_jaxpr/cond/branch_1_fun/all_gather | solution.py:59
  54.0 7.2 %convolution_convert_fusion = bf16[16,2304]{1,0:T(8,128)(2,1)S(1)} fusion(bf16[2304,2432]{1,0:T(8,128)(2,1)} %get-tuple-element.270, bf16[2432,16]{0,1:T(8,128)(2,1)S(1)} %reshape.83, f32[16]{0:T(128)S(1)} %add_rsqrt_fusion.2, f32[16]{0:T(128)S(1)} %broadcast_multiply_fusion, f32[2432]{0:T(1024)S(1)} %get-tuple-element.365, f32[2432]{0:T(1024)S(1)} %get-tuple-element.364), kind=kOutput, calls=%fused_computation.1 | convolution fusion | flops 179576832 | bytes 11377792 | tf_op jit(solution)/shard_map/while/body/eval_jaxpr/cond/branch_1_fun/dot_general | solution.py:92
  67.5 4.5 %all_gather.5 = bf16[16,1536]{1,0:T(8,128)(2,1)S(1)} all-gather(bf16[16,768]{1,0:T(8,128)(2,1)S(1)} %reshape.65), channel_id=1, replica_groups=mesh['cfg'=2,'section'=8,'patch'=2] {'patch'}, dimensions={1}, use_global_device_ids=true | all-gather | bytes 73728 | tf_op jit(solution)/shard_map/while/body/eval_jaxpr/cond/branch_1_fun/all_gather | solution.py:111
  76.3 5.0 %all-reduce = f32[16,64]{1,0:T(8,128)S(1)} all-reduce(f32[16,64]{1,0:T(8,128)S(1)} %fusion.54), channel_id=2, replica_groups=mesh['cfg'=2,'section'=8,'patch'=2] {'patch'}, use_global_device_ids=true, to_apply=%region_9.8.clone | all-reduce | flops 1024 | bytes 8192 | tf_op jit(solution)/shard_map/while/body/eval_jaxpr/cond
  83.7 34.7 %conditional.2 = (bf16[16,1216]{1,0:T(8,128)(2,1)}, bf16[64,12,128]{0,2,1:T(8,128)(2,1)S(1)}, f32[4,8,64]{2,1,0:T(8,128)S(1)}) conditional(s32[]{:T(128)} %convert_element_type.132, (bf16[64,12,128]{0,2,1:T(8,128)(2,1)S(1)}, f32[4,8,64]{2,1,0:T(8,128)S(1)}) %tuple.48, (s32[]{:T(128)}, s32[]{:T(128)}, bf16[4,16,64]{2,1,0:T(8,128)(2,1)S(1)}, ...), branch_computations={%region_1.1_spmd, %region_2.9_spmd} | conditional | flops 269630784 | bytes 21741536 | solution.py:155
  85.8 4.7 %all-gather = bf16[2,1216,16]{1,2,0:T(8,128)(2,1)S(1)} all-gather(bf16[1,1216,16]{1,2,0:T(8,128)(2,1)S(1)} %fusion.4), channel_id=1, replica_groups=mesh['cfg'=2,'section'=8,'patch'=2] {'patch'}, dimensions={0}, use_global_device_ids=true | all-gather | bytes 116736 | tf_op jit(solution)/shard_map/while/body/eval_jaxpr/cond/branch_1_fun/all_gather | solution.py:59
  91.1 7.2 %convolution_convert_fusion = bf16[16,2304]{1,0:T(8,128)(2,1)S(1)} fusion(bf16[2304,2432]{1,0:T(8,128)(2,1)} %get-tuple-element.270, bf16[2432,16]{0,1:T(8,128)(2,1)S(1)} %reshape.83, f32[16]{0:T(128)S(1)} %add_rsqrt_fusion.2, f32[16]{0:T(128)S(1)} %broadcast_multiply_fusion, f32[2432]{0:T(1024)S(1)} %get-tuple-element.365, f32[2432]{0:T(1024)S(1)} %get-tuple-element.364), kind=kOutput, calls=%fused_computation.1 | convolution fusion | flops 179576832 | bytes 11377792 | tf_op jit(solution)/shard_map/while/body/eval_jaxpr/cond/branch_1_fun/dot_general | solution.py:92
  99.4 3.8 dynamic_update_slice.4
  104.6 4.5 %all_gather.5 = bf16[16,1536]{1,0:T(8,128)(2,1)S(1)} all-gather(bf16[16,768]{1,0:T(8,128)(2,1)S(1)} %reshape.65), channel_id=1, replica_groups=mesh['cfg'=2,'section'=8,'patch'=2] {'patch'}, dimensions={1}, use_global_device_ids=true | all-gather | bytes 73728 | tf_op jit(solution)/shard_map/while/body/eval_jaxpr/cond/branch_1_fun/all_gather | solution.py:111
  113.4 5.0 %all-reduce = f32[16,64]{1,0:T(8,128)S(1)} all-reduce(f32[16,64]{1,0:T(8,128)S(1)} %fusion.54), channel_id=2, replica_groups=mesh['cfg'=2,'section'=8,'patch'=2] {'patch'}, use_global_device_ids=true, to_apply=%region_9.8.clone | all-reduce | flops 1024 | bytes 8192 | tf_op jit(solution)/shard_map/while/body/eval_jaxpr/cond
  120.8 34.7 %conditional.2 = (bf16[16,1216]{1,0:T(8,128)(2,1)}, bf16[64,12,128]{0,2,1:T(8,128)(2,1)S(1)}, f32[4,8,64]{2,1,0:T(8,128)S(1)}) conditional(s32[]{:T(128)} %convert_element_type.132, (bf16[64,12,128]{0,2,1:T(8,128)(2,1)S(1)}, f32[4,8,64]{2,1,0:T(8,128)S(1)}) %tuple.48, (s32[]{:T(128)}, s32[]{:T(128)}, bf16[4,16,64]{2,1,0:T(8,128)(2,1)S(1)}, ...), branch_computations={%region_1.1_spmd, %region_2.9_spmd} | conditional | flops 269630784 | bytes 21741536 | solution.py:155
  122.9 4.7 %all-gather = bf16[2,1216,16]{1,2,0:T(8,128)(2,1)S(1)} all-gather(bf16[1,1216,16]{1,2,0:T(8,128)(2,1)S(1)} %fusion.4), channel_id=1, replica_groups=mesh['cfg'=2,'section'=8,'patch'=2] {'patch'}, dimensions={0}, use_global_device_ids=true | all-gather | bytes 116736 | tf_op jit(solution)/shard_map/while/body/eval_jaxpr/cond/branch_1_fun/all_gather | solution.py:59
  128.1 7.2 %convolution_convert_fusion = bf16[16,2304]{1,0:T(8,128)(2,1)S(1)} fusion(bf16[2304,2432]{1,0:T(8,128)(2,1)} %get-tuple-element.270, bf16[2432,16]{0,1:T(8,128)(2,1)S(1)} %reshape.83, f32[16]{0:T(128)S(1)} %add_rsqrt_fusion.2, f32[16]{0:T(128)S(1)} %broadcast_multiply_fusion, f32[2432]{0:T(1024)S(1)} %get-tuple-element.365, f32[2432]{0:T(1024)S(1)} %get-tuple-element.364), kind=kOutput, calls=%fused_computation.1 | convolution fusion | flops 179576832 | bytes 11377792 | tf_op jit(solution)/shard_map/while/body/eval_jaxpr/cond/branch_1_fun/dot_general | solution.py:92
  136.4 3.8 dynamic_update_slice.4
  141.6 4.5 %all_gather.5 = bf16[16,1536]{1,0:T(8,128)(2,1)S(1)} all-gather(bf16[16,768]{1,0:T(8,128)(2,1)S(1)} %reshape.65), channel_id=1, replica_groups=mesh['cfg'=2,'section'=8,'patch'=2] {'patch'}, dimensions={1}, use_global_device_ids=true | all-gather | bytes 73728 | tf_op jit(solution)/shard_map/while/body/eval_jaxpr/cond/branch_1_fun/all_gather | solution.py:111
  150.4 5.0 %all-reduce = f32[16,64]{1,0:T(8,128)S(1)} all-reduce(f32[16,64]{1,0:T(8,128)S(1)} %fusion.54), channel_id=2, replica_groups=mesh['cfg'=2,'section'=8,'patch'=2] {'patch'}, use_global_device_ids=true, to_apply=%region_9.8.clone | all-reduce | flops 1024 | bytes 8192 | tf_op jit(solution)/shard_map/while/body/eval_jaxpr/cond
  158.4 34.2 %collective-permute-start = (bf16[16,1216]{1,0:T(8,128)(2,1)}, bf16[16,1216]{1,0:T(8,128)(2,1)S(1)}, u32[]{:S(2)}, u32[]{:S(2)}) collective-permute-start(bf16[16,1216]{1,0:T(8,128)(2,1)} %get-tuple-element.486), channel_id=1, source_target_pairs={{0,2},{2,4},{4,6},{6,8},{8,10},{10,12},{12,14},{1,3},{3,5},{5,7},{... | collective-permute-start | bytes 116744 | tf_op jit(solution)/shard_map/while/body/eval_jaxpr/ppermute | solution.py:17
  194.3 7.9 %collective-permute-start = (bf16[16,1216]{1,0:T(8,128)(2,1)}, bf16[16,1216]{1,0:T(8,128)(2,1)S(1)}, u32[]{:S(2)}, u32[]{:S(2)}) collective-permute-start(bf16[16,1216]{1,0:T(8,128)(2,1)} %get-tuple-element.486), channel_id=1, source_target_pairs={{0,2},{2,4},{4,6},{6,8},{8,10},{10,12},{12,14},{1,3},{3,5},{5,7},{... | collective-permute-start | bytes 116744 | tf_op jit(solution)/shard_map/while/body/eval_jaxpr/ppermute | solution.py:17
  203.8 38.5 %collective-permute-start = (bf16[16,1216]{1,0:T(8,128)(2,1)}, bf16[16,1216]{1,0:T(8,128)(2,1)S(1)}, u32[]{:S(2)}, u32[]{:S(2)}) collective-permute-start(bf16[16,1216]{1,0:T(8,128)(2,1)} %get-tuple-element.486), channel_id=1, source_target_pairs={{0,2},{2,4},{4,6},{6,8},{8,10},{10,12},{12,14},{1,3},{3,5},{5,7},{... | collective-permute-start | bytes 116744 | tf_op jit(solution)/shard_map/while/body/eval_jaxpr/ppermute | solution.py:17
  244.0 4.5 %collective-permute-start = (bf16[16,1216]{1,0:T(8,128)(2,1)}, bf16[16,1216]{1,0:T(8,128)(2,1)S(1)}, u32[]{:S(2)}, u32[]{:S(2)}) collective-permute-start(bf16[16,1216]{1,0:T(8,128)(2,1)} %get-tuple-element.486), channel_id=1, source_target_pairs={{0,2},{2,4},{4,6},{6,8},{8,10},{10,12},{12,14},{1,3},{3,5},{5,7},{... | collective-permute-start | bytes 116744 | tf_op jit(solution)/shard_map/while/body/eval_jaxpr/ppermute | solution.py:17
  250.2 30.3 %collective-permute-start = (bf16[16,1216]{1,0:T(8,128)(2,1)}, bf16[16,1216]{1,0:T(8,128)(2,1)S(1)}, u32[]{:S(2)}, u32[]{:S(2)}) collective-permute-start(bf16[16,1216]{1,0:T(8,128)(2,1)} %get-tuple-element.486), channel_id=1, source_target_pairs={{0,2},{2,4},{4,6},{6,8},{8,10},{10,12},{12,14},{1,3},{3,5},{5,7},{... | collective-permute-start | bytes 116744 | tf_op jit(solution)/shard_map/while/body/eval_jaxpr/ppermute | solution.py:17
  282.2 4.5 %collective-permute-start = (bf16[16,1216]{1,0:T(8,128)(2,1)}, bf16[16,1216]{1,0:T(8,128)(2,1)S(1)}, u32[]{:S(2)}, u32[]{:S(2)}) collective-permute-start(bf16[16,1216]{1,0:T(8,128)(2,1)} %get-tuple-element.486), channel_id=1, source_target_pairs={{0,2},{2,4},{4,6},{6,8},{8,10},{10,12},{12,14},{1,3},{3,5},{5,7},{... | collective-permute-start | bytes 116744 | tf_op jit(solution)/shard_map/while/body/eval_jaxpr/ppermute | solution.py:17
  288.3 36.3 %collective-permute-start = (bf16[16,1216]{1,0:T(8,128)(2,1)}, bf16[16,1216]{1,0:T(8,128)(2,1)S(1)}, u32[]{:S(2)}, u32[]{:S(2)}) collective-permute-start(bf16[16,1216]{1,0:T(8,128)(2,1)} %get-tuple-element.486), channel_id=1, source_target_pairs={{0,2},{2,4},{4,6},{6,8},{8,10},{10,12},{12,14},{1,3},{3,5},{5,7},{... | collective-permute-start | bytes 116744 | tf_op jit(solution)/shard_map/while/body/eval_jaxpr/ppermute | solution.py:17
  329.4 108.9 %psum.7 = f32[8,128]{1,0:T(8,128)S(1)} all-reduce(f32[8,128]{1,0:T(8,128)S(1)} %add_select_fusion), channel_id=1, replica_groups=mesh['cfg'=2,'section'=8,'patch'=2] {'section'}, use_global_device_ids=true, to_apply=%region_11.12 | all-reduce | flops 1024 | bytes 8192 | tf_op jit(solution)/shard_map/psum | solution.py:32
  (169 shorter events, 73.2 us)
Async XLA Ops:
  0.0 3.9 copy-start.1
  4.7 6.1 %slice-start = ((f32[1,1,3,2432]{3,1,2,0:T(1,128)}), f32[1,1,1,2432]{3,1,2,0:T(1,128)S(1)}, s32[]{:S(2)}) async-start(f32[1,1,3,2432]{3,1,2,0:T(1,128)} %param.16), calls=%async_computation | async-start | bytes 19456 | tf_op jit(solution)/shard_map/slice | solution.py:79
  4.7 6.2 %copy-start = (bf16[64,1216]{1,0:T(8,128)(2,1)S(1)}, bf16[64,1216]{1,0:T(8,128)(2,1)}, u32[]{:S(2)}) copy-start(bf16[64,1216]{1,0:T(8,128)(2,1)} %param.15) | copy-start | bytes 466948
  10.9 316.1 %copy-start.2 = (f32[4,16,64]{2,1,0:T(8,128)S(1)}, f32[4,16,64]{2,1,0:T(8,128)}, u32[]{:S(2)}) copy-start(f32[4,16,64]{2,1,0:T(8,128)} %param.14) | copy-start | bytes 49156
  44.3 2.4 collective-permute-start
  81.4 2.4 collective-permute-start
  118.4 2.4 collective-permute-start
  155.4 2.4 collective-permute-start
  158.4 35.2 %collective-permute-start = (bf16[16,1216]{1,0:T(8,128)(2,1)}, bf16[16,1216]{1,0:T(8,128)(2,1)S(1)}, u32[]{:S(2)}, u32[]{:S(2)}) collective-permute-start(bf16[16,1216]{1,0:T(8,128)(2,1)} %get-tuple-element.486), channel_id=1, source_target_pairs={{0,2},{2,4},{4,6},{6,8},{8,10},{10,12},{12,14},{1,3},{3,5},{5,7},{... | collective-permute-start | bytes 116744 | tf_op jit(solution)/shard_map/while/body/eval_jaxpr/ppermute | solution.py:17
  194.3 9.0 %collective-permute-start = (bf16[16,1216]{1,0:T(8,128)(2,1)}, bf16[16,1216]{1,0:T(8,128)(2,1)S(1)}, u32[]{:S(2)}, u32[]{:S(2)}) collective-permute-start(bf16[16,1216]{1,0:T(8,128)(2,1)} %get-tuple-element.486), channel_id=1, source_target_pairs={{0,2},{2,4},{4,6},{6,8},{8,10},{10,12},{12,14},{1,3},{3,5},{5,7},{... | collective-permute-start | bytes 116744 | tf_op jit(solution)/shard_map/while/body/eval_jaxpr/ppermute | solution.py:17
  203.8 39.6 %collective-permute-start = (bf16[16,1216]{1,0:T(8,128)(2,1)}, bf16[16,1216]{1,0:T(8,128)(2,1)S(1)}, u32[]{:S(2)}, u32[]{:S(2)}) collective-permute-start(bf16[16,1216]{1,0:T(8,128)(2,1)} %get-tuple-element.486), channel_id=1, source_target_pairs={{0,2},{2,4},{4,6},{6,8},{8,10},{10,12},{12,14},{1,3},{3,5},{5,7},{... | collective-permute-start | bytes 116744 | tf_op jit(solution)/shard_map/while/body/eval_jaxpr/ppermute | solution.py:17
  244.0 5.5 %collective-permute-start = (bf16[16,1216]{1,0:T(8,128)(2,1)}, bf16[16,1216]{1,0:T(8,128)(2,1)S(1)}, u32[]{:S(2)}, u32[]{:S(2)}) collective-permute-start(bf16[16,1216]{1,0:T(8,128)(2,1)} %get-tuple-element.486), channel_id=1, source_target_pairs={{0,2},{2,4},{4,6},{6,8},{8,10},{10,12},{12,14},{1,3},{3,5},{5,7},{... | collective-permute-start | bytes 116744 | tf_op jit(solution)/shard_map/while/body/eval_jaxpr/ppermute | solution.py:17
  250.2 31.4 %collective-permute-start = (bf16[16,1216]{1,0:T(8,128)(2,1)}, bf16[16,1216]{1,0:T(8,128)(2,1)S(1)}, u32[]{:S(2)}, u32[]{:S(2)}) collective-permute-start(bf16[16,1216]{1,0:T(8,128)(2,1)} %get-tuple-element.486), channel_id=1, source_target_pairs={{0,2},{2,4},{4,6},{6,8},{8,10},{10,12},{12,14},{1,3},{3,5},{5,7},{... | collective-permute-start | bytes 116744 | tf_op jit(solution)/shard_map/while/body/eval_jaxpr/ppermute | solution.py:17
  282.2 5.5 %collective-permute-start = (bf16[16,1216]{1,0:T(8,128)(2,1)}, bf16[16,1216]{1,0:T(8,128)(2,1)S(1)}, u32[]{:S(2)}, u32[]{:S(2)}) collective-permute-start(bf16[16,1216]{1,0:T(8,128)(2,1)} %get-tuple-element.486), channel_id=1, source_target_pairs={{0,2},{2,4},{4,6},{6,8},{8,10},{10,12},{12,14},{1,3},{3,5},{5,7},{... | collective-permute-start | bytes 116744 | tf_op jit(solution)/shard_map/while/body/eval_jaxpr/ppermute | solution.py:17
  288.3 37.4 %collective-permute-start = (bf16[16,1216]{1,0:T(8,128)(2,1)}, bf16[16,1216]{1,0:T(8,128)(2,1)S(1)}, u32[]{:S(2)}, u32[]{:S(2)}) collective-permute-start(bf16[16,1216]{1,0:T(8,128)(2,1)} %get-tuple-element.486), channel_id=1, source_target_pairs={{0,2},{2,4},{4,6},{6,8},{8,10},{10,12},{12,14},{1,3},{3,5},{5,7},{... | collective-permute-start | bytes 116744 | tf_op jit(solution)/shard_map/while/body/eval_jaxpr/ppermute | solution.py:17
  325.7 3.6 collective-permute-start.1
where the time goes:
time: 440 us; the launch traced here: 439 us
  blocking collectives  167 us (38%)
  starting transfers between devices  163 us (37%)
  matrix products  50.1 us (11%)
  local copies, waits for them, and re-layouts  36.9 us (8%)
  waiting for transfers between devices  12.4 us (3%)
  other arithmetic  5.46 us (1%)
    ppermute x11, starting transfers between devices, from_behind(): lax.ppermute(value, axis, [(source, source + steps) for source in range(l...  161 us
    psum x1, blocking collectives, broadcast(): return lax.psum(kept, axis)  109 us
    dot_general x4, matrix products, block_work(): lax.dot_general(normed, w_proj, (((1,), (1,)), ((), ())), preferred_eleme...  28.8 us
    cond x4, blocking collectives  20.1 us
    all_gather x4, blocking collectives, widen(): return lax.all_gather(column_rows, 'patch', axis=1, tiled=True)  19.8 us
    all_gather x4, blocking collectives, block_work(): lax.all_gather(attended, 'patch', axis=1, tiled=True)  18 us
    dot_general x4, matrix products, block_work(): jnp.dot(lax.all_gather(attended, 'patch', axis=1, tiled=True), w_back, pr...  13.4 us
    dynamic_update_slice x4, local copies, waits for them, and re-layouts, block_work(): lax.dynamic_update_slice(buffer, new_pair, (micro_index * batch_rows, zer...  12.9 us
  transfers between devices with their start and end apart: 12, of which 12 were waited for; matrix products, arithmetic and copies ran while one was open for 0% of the time, Pallas kernels for 0%

commit v1 on v0

v1 whole, which is shorter than its diff:
```python
import functools

import jax
import jax.numpy as jnp
from jax import lax
from jax.experimental import pallas as pl
from jax.experimental.pallas import tpu as pltpu
from jax.sharding import PartitionSpec as P

HEAD_DIM = 64
STEPS = 28
SHIFT_SIGMA = 3.0
EPS_NORM = 1e-06
MESH = pl.DeviceIdType.MESH
BF16 = jnp.bfloat16
F32 = jnp.float32


def sigma_at(position):
    level = 1.0 - position.astype(F32) / STEPS
    return SHIFT_SIGMA * level / (1.0 + (SHIFT_SIGMA - 1.0) * level)


def patch_of(index, micro_count, batch_rows):
    patch = jnp.zeros_like(index)
    for m in range(1, micro_count):
        patch = patch + jnp.where(index >= m * batch_rows, 1, 0)
    return patch


def kernel(
    dims,
    latent_ref, w_in_ref, mod_ref, gate_ref, kv_ref, w_final_ref, guide_ref, w_qkv_hbm, w_out_hbm,
    out_ref,
    w_qkv, w_out, xbuf, xfull, normed, keys, values_t, mask_old, mask_new, att_t, att_all, newx,
    speed, speeds, guided,
    w_sem, wo_sem, e_send, x_send, x_recv, a_send, a_recv, v_send, v_recv, g_send, g_recv,
):
    branches, sections, patches, groups, micro_count, batch_rows, img, txt = dims
    b, s, p = lax.axis_index("cfg"), lax.axis_index("section"), lax.axis_index("patch")
    last = sections - 1
    rows, columns = newx.shape
    heads, old, _ = kv_ref.shape
    group_heads = heads // groups
    group_inner = group_heads * HEAD_DIM
    half = micro_count // branches

    def weight_copy(c, g):
        part = pl.ds(g * group_inner, group_inner)
        return pltpu.make_async_copy(w_qkv_hbm.at[c, part], w_qkv.at[c, part], w_sem.at[c, g])

    for g in range(groups):
        for c in range(3):
            weight_copy(c, g).start()
    out_copy = pltpu.make_async_copy(w_out_hbm, w_out, wo_sem)
    out_copy.start()

    others = [lax.rem(p + d, patches) for d in range(1, patches)]

    barrier = pltpu.get_barrier_semaphore()
    for q in others:
        pl.semaphore_signal(barrier, inc=1, device_id={"patch": q}, device_id_type=MESH)

    @pl.when(s > 0)
    def _():
        for q in range(patches):
            pl.semaphore_signal(
                barrier, inc=1, device_id={"section": s - 1, "patch": q}, device_id_type=MESH
            )

    @pl.when(s < last)
    def _():
        pl.semaphore_signal(barrier, inc=1, device_id={"section": last}, device_id_type=MESH)

    @pl.when(s == last)
    def _():
        for e in range(1, branches):
            for q in range(patches):
                pl.semaphore_signal(
                    barrier, inc=1, device_id={"cfg": lax.rem(b + e, branches), "patch": q},
                    device_id_type=MESH,
                )

    @pl.when(s < last)
    def _():
        pl.semaphore_wait(barrier, 2 * patches - 1)

    @pl.when(s == last)
    def _():
        pl.semaphore_wait(barrier, branches * patches - 1 + last)

    def x_copy(source, q, sems, target):
        return pltpu.make_async_remote_copy(
            src_ref=source, dst_ref=xbuf.at[p], send_sem=sems.at[q], recv_sem=x_recv.at[p],
            device_id=target, device_id_type=MESH,
        )

    def x_arrival(q):
        return pltpu.make_async_remote_copy(
            src_ref=newx, dst_ref=xbuf.at[q], send_sem=x_send.at[0], recv_sem=x_recv.at[q],
            device_id={"patch": others[0]}, device_id_type=MESH,
        )

    @pl.when(s == 0)
    def _():
        embedded = jnp.dot(latent_ref[...], w_in_ref[...], preferred_element_type=F32)
        xbuf[p] = embedded.astype(BF16)
        for q in others:
            x_copy(xbuf.at[p], q, e_send, {"patch": q}).start()

    row_patch = patch_of(lax.broadcasted_iota(jnp.int32, (old, rows), 1), micro_count, batch_rows)
    key_index = lax.broadcasted_iota(jnp.int32, (old, rows), 0)
    key_patch = patch_of(key_index, micro_count, batch_rows)
    is_text = (key_index >= img) & (key_index < img + txt)
    is_stale = (key_index < img) & (key_patch > row_patch)
    mask_old[...] = jnp.where(is_text | is_stale, 1.0, 0.0)
    row_patch = patch_of(lax.broadcasted_iota(jnp.int32, (rows, rows), 1), micro_count, batch_rows)
    key_patch = patch_of(lax.broadcasted_iota(jnp.int32, (rows, rows), 0), micro_count, batch_rows)
    mask_new[...] = jnp.where(key_patch <= row_patch, 1.0, 0.0)

    @pl.loop(0, heads)
    def _(h):
        pair = kv_ref[h].astype(F32)
        key = pair[:, :HEAD_DIM]
        scale = lax.rsqrt(jnp.mean(key * key, axis=-1, keepdims=True) + EPS_NORM)
        keys[h] = (key * scale).astype(BF16)
        values_t[h] = pair.T[HEAD_DIM:].astype(BF16)

    @pl.when(s == 0)
    def _():
        for q in others:
            x_arrival(q).wait_recv()

    @pl.when(s > 0)
    def _():
        for q in range(patches):
            x_arrival(q).wait_recv()

    for q in range(patches):
        xfull[:, q * columns : (q + 1) * columns] = xbuf[q].astype(F32)
    x = xfull[...]
    centred = x - jnp.mean(x, axis=-1, keepdims=True)
    var = jnp.mean(centred * centred, axis=-1, keepdims=True)
    unit = centred * lax.rsqrt(var + EPS_NORM)
    normed[...] = (unit * (1.0 + mod_ref[1:2]) + mod_ref[0:1]).astype(BF16)

    def att_copy(g, q):
        return pltpu.make_async_remote_copy(
            src_ref=att_all.at[p, g], dst_ref=att_all.at[p, g], send_sem=a_send.at[q, g],
            recv_sem=a_recv.at[p, g], device_id={"patch": q}, device_id_type=MESH,
        )

    def att_arrival(g, q):
        return pltpu.make_async_remote_copy(
            src_ref=att_all.at[q, g], dst_ref=att_all.at[q, g], send_sem=a_send.at[q, g],
            recv_sem=a_recv.at[q, g], device_id={"patch": q}, device_id_type=MESH,
        )

    for g in range(groups):
        projected = []
        for c in range(3):
            weight_copy(c, g).wait()
            product = lax.dot_general(
                w_qkv[c, g * group_inner : (g + 1) * group_inner], normed[...],
                (((1,), (1,)), ((), ())), preferred_element_type=F32,
            )
            projected.append(product.astype(BF16).reshape(group_heads, HEAD_DIM, rows))
        scaled = []
        for c in range(2):
            part = projected[c].astype(F32)
            scale = lax.rsqrt(jnp.mean(part * part, axis=1, keepdims=True) + EPS_NORM)
            scaled.append((part * scale).astype(BF16))
        for j in range(group_heads):
            h = g * group_heads + j
            query = scaled[0][j] * BF16(HEAD_DIM**-0.5)
            score_old = jnp.dot(keys[h], query, preferred_element_type=F32)
            score_new = lax.dot_general(
                scaled[1][j], query, (((0,), (0,)), ((), ())), preferred_element_type=F32
            )
            power_old = jnp.exp(score_old) * mask_old[...]
            power_new = jnp.exp(score_new) * mask_new[...]
            total = jnp.sum(power_old, axis=0, keepdims=True) + jnp.sum(
                power_new, axis=0, keepdims=True
            )
            share = 1.0 / total
            att = jnp.dot(values_t[h], (power_old * share).astype(BF16), preferred_element_type=F32)
            att += jnp.dot(
                projected[2][j], (power_new * share).astype(BF16), preferred_element_type=F32
            )
            att_t[j * HEAD_DIM : (j + 1) * HEAD_DIM] = att
        att_all[p, g] = att_t[...].T.astype(BF16)
        for q in others:
            att_copy(g, q).start()

    out_copy.wait()

    def out_part(q, g):
        start = pl.multiple_of(q * (groups * group_inner) + g * group_inner, group_inner)
        return jnp.dot(
            att_all[q, g], w_out[pl.ds(start, group_inner)], preferred_element_type=F32
        )

    update = out_part(p, 0)
    for g in range(1, groups):
        update += out_part(p, g)
    for g in range(groups):
        for q in others:
            att_arrival(g, q).wait_recv()
            update += out_part(q, g)
    newx[...] = (xbuf[p].astype(F32) + gate_ref[...] * update).astype(BF16)

    @pl.when(s < last)
    def _():
        for q in range(patches):
            x_copy(newx, q, x_send, {"section": s + 1, "patch": q}).start()

    def v_copy(e, q):
        return pltpu.make_async_remote_copy(
            src_ref=speed.at[pl.ds(e * half, half), q], dst_ref=speeds.at[b, p],
            send_sem=v_send.at[e, q], recv_sem=v_recv.at[b, p],
            device_id={"cfg": e, "patch": q}, device_id_type=MESH,
        )

    def v_arrival(e, q):
        return pltpu.make_async_remote_copy(
            src_ref=speed.at[pl.ds(0, half), q], dst_ref=speeds.at[e, q],
            send_sem=v_send.at[e, q], recv_sem=v_recv.at[e, q],
            device_id={"cfg": e, "patch": q}, device_id_type=MESH,
        )

    def g_copy(t):
        return pltpu.make_async_remote_copy(
            src_ref=guided, dst_ref=guided, send_sem=g_send.at[t], recv_sem=g_recv,
            device_id={"section": t}, device_id_type=MESH,
        )

    @pl.when(s == last)
    def _():
        partial = jnp.dot(newx[...], w_final_ref[...], preferred_element_type=F32)
        speed[...] = partial.reshape(speed.shape)
        peers = []
        for e in range(branches):
            for d in range(patches):
                if e or d:
                    peers.append((lax.rem(b + e, branches), lax.rem(p + d, patches)))
        for e, q in peers:
            v_copy(e, q).start()
        speeds[b, p] = speed[pl.ds(b * half, half), p]
        for e, q in peers:
            v_arrival(e, q).wait_recv()
        conditional = jnp.sum(speeds[0], axis=0)
        unconditional = jnp.sum(speeds[1], axis=0)
        guided[...] = unconditional + guide_ref[0] * (conditional - unconditional)
        for t in range(last):
            g_copy(t).start()
        for e, q in peers:
            v_copy(e, q).wait_send()
        for t in range(last):
            g_copy(t).wait_send()

    @pl.when(s == 0)
    def _():
        for q in others:
            x_copy(xbuf.at[p], q, e_send, {"patch": q}).wait_send()

    for g in range(groups):
        for q in others:
            att_copy(g, q).wait_send()

    @pl.when(s < last)
    def _():
        for q in range(patches):
            x_copy(newx, q, x_send, {"section": s + 1, "patch": q}).wait_send()
        g_copy(s).wait_recv()

    out_ref[...] = guided[...]


def on_device(
    latent, w_in, modulation, w_qkv, text_kv, stale_kv, w_out, w_final, guidance, step_index
):
    branches, sections = lax.axis_size("cfg"), lax.axis_size("section")
    patches = lax.axis_size("patch")
    b, s, p = lax.axis_index("cfg"), lax.axis_index("section"), lax.axis_index("patch")
    micro_count, batch_rows, chan = latent.shape
    rows = micro_count * batch_rows
    own_rows = batch_rows // patches
    columns = w_in.shape[1]
    width = columns * patches
    local_inner = w_qkv.shape[2]
    heads = local_inner // HEAD_DIM
    inner = w_out.shape[1]
    txt, img = text_kv.shape[2], stale_kv.shape[2]
    old = -(-(txt + img) // 16) * 16
    half = micro_count // branches
    groups = next(g for g in (3, 2, 1) if g == 1 or local_inner % (g * 128) == 0)
    group_inner = local_inner // groups

    joined = jnp.concatenate([stale_kv[0, 0], text_kv[0, 0]], axis=0)
    joined = jnp.pad(joined, ((0, old - txt - img), (0, 0), (0, 0)))
    kv = jnp.transpose(joined, (1, 0, 2))
    mod = modulation[0, 0]
    gate = lax.dynamic_slice_in_dim(mod[2:3], p * columns, columns, 1)

    dims = (branches, sections, patches, groups, micro_count, batch_rows, img, txt)
    vmem = pl.BlockSpec(memory_space=pltpu.VMEM)
    dma = pltpu.SemaphoreType.DMA
    guided = pl.pallas_call(
        functools.partial(kernel, dims),
        out_shape=jax.ShapeDtypeStruct((half, own_rows, chan), F32),
        in_specs=[vmem] * 6
        + [pl.BlockSpec(memory_space=pltpu.SMEM)]
        + [pl.BlockSpec(memory_space=pl.ANY)] * 2,
        out_specs=vmem,
        scratch_shapes=[
            pltpu.VMEM((3, local_inner, width), BF16),
            pltpu.VMEM((inner, columns), BF16),
            pltpu.VMEM((patches, rows, columns), BF16),
            pltpu.VMEM((rows, width), F32),
            pltpu.VMEM((rows, width), BF16),
            pltpu.VMEM((heads, old, HEAD_DIM), BF16),
            pltpu.VMEM((heads, HEAD_DIM, old), BF16),
            pltpu.VMEM((old, rows), F32),
            pltpu.VMEM((rows, rows), F32),
            pltpu.VMEM((group_inner, rows), F32),
            pltpu.VMEM((patches, groups, rows, group_inner), BF16),
            pltpu.VMEM((rows, columns), BF16),
            pltpu.VMEM((micro_count, patches, own_rows, chan), F32),
            pltpu.VMEM((branches, patches, half, own_rows, chan), F32),
            pltpu.VMEM((half, own_rows, chan), F32),
            dma((3, groups)),
            dma,
            dma((patches,)),
            dma((patches,)),
            dma((patches,)),
            dma((patches, groups)),
            dma((patches, groups)),
            dma((branches, patches)),
            dma((branches, patches)),
            dma((sections,)),
            dma,
        ],
        compiler_params=pltpu.CompilerParams(
            collective_id=0, has_side_effects=True, vmem_limit_bytes=48 * 1024 * 1024
        ),
    )(
        latent.astype(BF16).reshape(rows, chan), w_in, mod, gate, kv, w_final, guidance,
        w_qkv[0], w_out[0],
    )

    section_width = half * chan // sections
    flat_guided = jnp.transpose(guided, (1, 0, 2)).reshape(own_rows, half * chan)
    own_latent = lax.dynamic_slice(
        latent, (b * half, p * own_rows, 0), (half, own_rows, chan)
    )
    flat_latent = jnp.transpose(own_latent, (1, 0, 2)).reshape(own_rows, half * chan)
    step_size = sigma_at(step_index[0] + 1) - sigma_at(step_index[0])
    result = flat_latent + step_size * flat_guided
    return lax.dynamic_slice_in_dim(result, s * section_width, section_width, 1)


def solution(mesh):
    in_specs = (
        P(),
        P(None, "patch"),
        P("section", "cfg", None, None),
        P("section", None, "patch", None),
        P("section", "cfg", None, "patch", None),
        P("section", "cfg", None, "patch", None),
        P("section", None, "patch"),
        P("patch", None),
        P(),
        P(),
    )
    out_specs = P("patch", ("cfg", "section"))
    return jax.shard_map(
        on_device, mesh=mesh, in_specs=in_specs, out_specs=out_specs, check_vma=False
    )
```

time: 440 us -> 166 us (0.38)
  blocking collectives: 167 us -> 0 us
  starting transfers between devices: 163 us -> 0 us
  Pallas kernels: 0 us -> 153 us
  matrix products: 50.1 us -> 0 us
  local copies, waits for them, and re-layouts: 36.9 us -> 10.9 us
  waiting for transfers between devices: 12.4 us -> 0 us
  other arithmetic: 5.46 us -> 0.11 us
    ppermute x12 -> x0, starting transfers between devices: 163 us -> none  [the longest x11 161 us: from_behind(): lax.ppermute(value, axis, [(source, source + steps) for source in range(l...]
    pallas_call x0 -> x1, Pallas kernels: none -> 153 us  [on_device(): pl.pallas_call(functools.partial(kernel, dims), out_shape=jax.ShapeDtypeS...]
    psum x1 -> x0, blocking collectives: 109 us -> none  [broadcast(): return lax.psum(kept, axis)]
    dot_general x20 -> x0, matrix products: 48 us -> none  [the longest x4 28.8 us: block_work(): lax.dot_general(normed, w_proj, (((1,), (1,)), ((), ())), preferred_eleme...]
    all_gather x8 -> x0, blocking collectives: 37.8 us -> none  [the longest x4 19.8 us: widen(): return lax.all_gather(column_rows, 'patch', axis=1, tiled=True)]
    cond x4 -> x0, blocking collectives: 20.1 us -> none
    dynamic_update_slice x4 -> x0, local copies, waits for them, and re-layouts: 12.9 us -> none  [block_work(): lax.dynamic_update_slice(buffer, new_pair, (micro_index * batch_rows, zer...]
    ppermute x12 -> x0, waiting for transfers between devices: 12.4 us -> none  [the longest x11 11.6 us: from_behind(): lax.ppermute(value, axis, [(source, source + steps) for source in range(l...]
  transfers between devices with their start and end apart: 12 -> 0, of which waited for: 12 -> 0; matrix products, arithmetic and copies ran while one was open for 0% -> 0% of each run, Pallas kernels for 0% -> 0%
where the time goes in v1:
time: 166 us
  Pallas kernels  153 us (92%)
  local copies, waits for them, and re-layouts  10.9 us (7%)
    pallas_call x1, Pallas kernels, on_device(): pl.pallas_call(functools.partial(kernel, dims), out_shape=jax.ShapeDtypeS...  153 us
    unnamed x17, local copies, waits for them, and re-layouts  9.34 us

profile of v1, /device:TPU:0, one launch (start us, length us, event | category | flops | bytes accessed | tf_op | source)
XLA Modules:
  0.0 165.9 jit_solution(13797108927451956714)
XLA Ops:
  0.0 0.7 slice.4
  0.7 0.1 dynamic-slice_bitcast_fusion.gate_ref
  0.8 0.0 copy-start.2
  0.8 0.0 copy-start.3
  0.8 6.2 %copy.13 = bf16[1,1536,1216]{2,1,0:T(8,128)(2,1)} copy(bf16[1,1536,1216]{1,2,0:T(8,128)(2,1)} %param.16) | data formatting | bytes 7471104 | tf_op args[6]
  7.0 0.0 copy-start.4
  7.0 0.0 copy-start.5
  7.0 0.0 copy-start.6
  7.0 0.0 copy-start.1
  7.0 0.0 copy-done.2
  7.0 0.0 copy-done.3
  7.0 0.1 fusion.3.kv_ref
  7.1 0.8 copy-done.4
  7.9 0.2 copy.14.w_final_ref
  8.1 0.0 copy-done.5
  8.2 0.0 copy-done.6
  8.8 0.0 copy-done.1
  8.8 0.0 copy-start
  8.8 2.1 %copy-done = bf16[1,1536,1216]{2,1,0:T(8,128)(2,1)S(1)} copy-done((bf16[1,1536,1216]{2,1,0:T(8,128)(2,1)S(1)}, bf16[1,1536,1216]{2,1,0:T(8,128)(2,1)}, u32[]{:S(2)}) %copy-start) | copy-done | bytes 3735576
  11.0 153.4 %shard_map.100 = f32[2,8,64]{2,1,0:T(8,128)S(1)} custom-call(bf16[64,64]{1,0:T(8,128)(2,1)S(1)} %bitcast.17, bf16[64,1216]{1,0:T(8,128)(2,1)S(1)} %copy-done.1, f32[3,2432]{1,0:T(4,128)S(1)} %bitcast.16, f32[1,1216]{1,0:T(1,128)S(1)} %dynamic-slice_bitcast_fusion.gate_ref, bf16[12,400,128]{2,1,0:T(8,128)(2,1)S(1)} %fusion.3.kv_ref, ...), custom_call_target="tpu_custom_call" | custom-call | tf_op jit(solution)/shard_map/pallas_call | solution.py:308
  165.1 0.1 add.41
  165.2 0.7 constant_dynamic-slice_fusion
  (4 shorter events, 0.0 us)
Async XLA Ops:
  0.8 6.2 %copy-start.2 = (bf16[1,1,333,12,128]{4,2,3,1,0:T(8,128)(2,1)S(1)}, bf16[1,1,333,12,128]{4,2,3,1,0:T(8,128)(2,1)}, u32[]{:S(2)}) copy-start(bf16[1,1,333,12,128]{4,2,3,1,0:T(8,128)(2,1)} %param.14) | copy-start | bytes 3068932
  0.8 6.2 %copy-start.3 = (bf16[1,1,64,12,128]{4,2,3,1,0:T(8,128)(2,1)S(1)}, bf16[1,1,64,12,128]{4,2,3,1,0:T(8,128)(2,1)}, u32[]{:S(2)}) copy-start(bf16[1,1,64,12,128]{4,2,3,1,0:T(8,128)(2,1)} %param.15) | copy-start | bytes 589828
  7.0 0.9 copy-start.4
  7.0 1.1 copy-start.5
  7.0 1.2 copy-start.6
  7.0 1.8 %copy-start.1 = (bf16[64,1216]{1,0:T(8,128)(2,1)S(1)}, bf16[64,1216]{1,0:T(8,128)(2,1)}, u32[]{:S(2)}) copy-start(bf16[64,1216]{1,0:T(8,128)(2,1)} %w_in_ref.1) | copy-start | bytes 466948
  8.8 2.1 %copy-start = (bf16[1,1536,1216]{2,1,0:T(8,128)(2,1)S(1)}, bf16[1,1536,1216]{2,1,0:T(8,128)(2,1)}, u32[]{:S(2)}) copy-start(bf16[1,1536,1216]{2,1,0:T(8,128)(2,1)} %copy.13) | copy-start | bytes 11206660

commit v2 on v1

--- a/solution.py
+++ b/solution.py
@@ -32,11 +32,11 @@
     dims,
     latent_ref, w_in_ref, mod_ref, gate_ref, kv_ref, w_final_ref, guide_ref, w_qkv_hbm, w_out_hbm,
     out_ref,
-    w_qkv, w_out, xbuf, xfull, normed, keys, values_t, mask_old, mask_new, att_t, att_all, newx,
+    w_qkv, w_out, xbuf, xfull, normed, keys, values_t, mask_old, mask_new, att_all, newx,
     speed, speeds, guided,
     w_sem, wo_sem, e_send, x_send, x_recv, a_send, a_recv, v_send, v_recv, g_send, g_recv,
 ):
-    branches, sections, patches, groups, micro_count, batch_rows, img, txt = dims
+    branches, sections, patches, groups, micro_count, batch_rows, img, txt, out_turned = dims
     b, s, p = lax.axis_index("cfg"), lax.axis_index("section"), lax.axis_index("patch")
     last = sections - 1
     rows, columns = newx.shape
@@ -170,25 +170,28 @@
             part = projected[c].astype(F32)
             scale = lax.rsqrt(jnp.mean(part * part, axis=1, keepdims=True) + EPS_NORM)
             scaled.append((part * scale).astype(BF16))
+        scores = []
         for j in range(group_heads):
-            h = g * group_heads + j
             query = scaled[0][j] * BF16(HEAD_DIM**-0.5)
-            score_old = jnp.dot(keys[h], query, preferred_element_type=F32)
+            score_old = jnp.dot(keys[g * group_heads + j], query, preferred_element_type=F32)
             score_new = lax.dot_general(
                 scaled[1][j], query, (((0,), (0,)), ((), ())), preferred_element_type=F32
             )
-            power_old = jnp.exp(score_old) * mask_old[...]
-            power_new = jnp.exp(score_new) * mask_new[...]
-            total = jnp.sum(power_old, axis=0, keepdims=True) + jnp.sum(
-                power_new, axis=0, keepdims=True
-            )
-            share = 1.0 / total
-            att = jnp.dot(values_t[h], (power_old * share).astype(BF16), preferred_element_type=F32)
-            att += jnp.dot(
-                projected[2][j], (power_new * share).astype(BF16), preferred_element_type=F32
-            )
-            att_t[j * HEAD_DIM : (j + 1) * HEAD_DIM] = att
-        att_all[p, g] = att_t[...].T.astype(BF16)
+            scores.append((score_old, score_new))
+        powers = [(jnp.exp(so) * mask_old[...], jnp.exp(sn) * mask_new[...]) for so, sn in scores]
+        shares = [
+            1.0 / (jnp.sum(po, axis=0, keepdims=True) + jnp.sum(pn, axis=0, keepdims=True))
+            for po, pn in powers
+        ]
+        parts = []
+        for j in range(group_heads):
+            weights_old = (powers[j][0] * shares[j]).astype(BF16)
+            weights_new = (powers[j][1] * shares[j]).astype(BF16)
+            parts.append(
+                jnp.dot(values_t[g * group_heads + j], weights_old, preferred_element_type=F32)
+                + jnp.dot(projected[2][j], weights_new, preferred_element_type=F32)
+            )
+        att_all[p, g] = jnp.concatenate(parts, axis=0).T.astype(BF16)
         for q in others:
             att_copy(g, q).start()
 
@@ -196,6 +199,11 @@
 
     def out_part(q, g):
         start = pl.multiple_of(q * (groups * group_inner) + g * group_inner, group_inner)
+        if out_turned:
+            return lax.dot_general(
+                att_all[q, g], w_out[:, pl.ds(start, group_inner)], (((1,), (1,)), ((), ())),
+                preferred_element_type=F32,
+            )
         return jnp.dot(
             att_all[q, g], w_out[pl.ds(start, group_inner)], preferred_element_type=F32
         )
@@ -236,7 +244,9 @@
 
     @pl.when(s == last)
     def _():
-        partial = jnp.dot(newx[...], w_final_ref[...], preferred_element_type=F32)
+        partial = lax.dot_general(
+            newx[...], w_final_ref[...], (((1,), (1,)), ((), ())), preferred_element_type=F32
+        )
         speed[...] = partial.reshape(speed.shape)
         peers = []
         for e in range(branches):
@@ -302,7 +312,10 @@
     mod = modulation[0, 0]
     gate = lax.dynamic_slice_in_dim(mod[2:3], p * columns, columns, 1)
 
-    dims = (branches, sections, patches, groups, micro_count, batch_rows, img, txt)
+    out_turned = group_inner % 128 == 0
+    dims = (
+        branches, sections, patches, groups, micro_count, batch_rows, img, txt, out_turned
+    )
     vmem = pl.BlockSpec(memory_space=pltpu.VMEM)
     dma = pltpu.SemaphoreType.DMA
     guided = pl.pallas_call(
@@ -314,7 +327,7 @@
         out_specs=vmem,
         scratch_shapes=[
             pltpu.VMEM((3, local_inner, width), BF16),
-            pltpu.VMEM((inner, columns), BF16),
+            pltpu.VMEM((columns, inner) if out_turned else (inner, columns), BF16),
             pltpu.VMEM((patches, rows, columns), BF16),
             pltpu.VMEM((rows, width), F32),
             pltpu.VMEM((rows, width), BF16),
@@ -322,7 +335,6 @@
             pltpu.VMEM((heads, HEAD_DIM, old), BF16),
             pltpu.VMEM((old, rows), F32),
             pltpu.VMEM((rows, rows), F32),
-            pltpu.VMEM((group_inner, rows), F32),
             pltpu.VMEM((patches, groups, rows, group_inner), BF16),
             pltpu.VMEM((rows, columns), BF16),
             pltpu.VMEM((micro_count, patches, own_rows, chan), F32),
@@ -344,8 +356,8 @@
             collective_id=0, has_side_effects=True, vmem_limit_bytes=48 * 1024 * 1024
         ),
     )(
-        latent.astype(BF16).reshape(rows, chan), w_in, mod, gate, kv, w_final, guidance,
-        w_qkv[0], w_out[0],
+        latent.astype(BF16).reshape(rows, chan), w_in, mod, gate, kv, w_final.T, guidance,
+        w_qkv[0], w_out[0].T if out_turned else w_out[0],
     )
 
     section_width = half * chan // sections

time: 166 us -> 141 us (0.85)
  Pallas kernels: 153 us -> 134 us
  local copies, waits for them, and re-layouts: 10.9 us -> 3.67 us
    pallas_call x1, Pallas kernels: 153 us -> 134 us  [on_device(): pl.pallas_call(functools.partial(kernel, dims), out_shape=jax.ShapeDtypeS...]
    unnamed x17 -> x11, local copies, waits for them, and re-layouts: 9.34 us -> 2.08 us
where the time goes in v2:
time: 141 us
  Pallas kernels  134 us (95%)
  local copies, waits for them, and re-layouts  3.67 us (3%)
  between operations  1.48 us (1%)
    pallas_call x1, Pallas kernels, on_device(): pl.pallas_call(functools.partial(kernel, dims), out_shape=jax.ShapeDtypeS...  134 us

profile of v2, /device:TPU:0, one launch (start us, length us, event | category | flops | bytes accessed | tf_op | source)
XLA Modules:
  0.0 140.9 jit_solution(7793700640669528077)
XLA Ops:
  0.0 0.0 copy-start.3
  0.0 0.0 copy-start.4
  0.0 0.0 copy-start.2
  0.0 0.0 copy-start.1
  0.0 0.8 slice.4
  0.8 0.1 dynamic-slice_bitcast_fusion.gate_ref
  0.9 1.3 fusion.3.kv_ref
  2.2 0.0 copy-done.3
  2.2 0.0 copy-done.4
  2.9 0.0 copy-done.2
  2.9 0.0 copy-done.1
  2.9 0.0 copy-start
  2.9 2.0 %copy-done = bf16[1,1536,1216]{1,2,0:T(8,128)(2,1)S(1)} copy-done((bf16[1,1536,1216]{1,2,0:T(8,128)(2,1)S(1)}, bf16[1,1536,1216]{1,2,0:T(8,128)(2,1)}, u32[]{:S(2)}) %copy-start) | copy-done | bytes 3735576
  5.0 134.4 %shard_map.100 = f32[2,8,64]{2,1,0:T(8,128)S(1)} custom-call(bf16[64,64]{1,0:T(8,128)(2,1)S(1)} %bitcast.21, bf16[64,1216]{1,0:T(8,128)(2,1)S(1)} %copy-done.1, f32[3,2432]{1,0:T(4,128)S(1)} %bitcast.20, f32[1,1216]{1,0:T(1,128)S(1)} %dynamic-slice_bitcast_fusion.gate_ref, bf16[12,400,128]{2,1,0:T(8,128)(2,1)S(1)} %fusion.3.kv_ref, ...), custom_call_target="tpu_custom_call" | custom-call | tf_op jit(solution)/shard_map/pallas_call | solution.py:321
  140.2 0.1 add.41
  140.2 0.7 constant_dynamic-slice_fusion
  (4 shorter events, 0.0 us)
Async XLA Ops:
  0.0 2.2 %copy-start.3 = (f32[1,1,3,2432]{3,1,2,0:T(1,128)S(1)}, f32[1,1,3,2432]{3,1,2,0:T(1,128)}, u32[]{:S(2)}) copy-start(f32[1,1,3,2432]{3,1,2,0:T(1,128)} %param.12) | copy-start | bytes 87556
  0.0 2.2 %copy-start.4 = (f32[4,16,64]{2,1,0:T(8,128)S(1)}, f32[4,16,64]{2,1,0:T(8,128)}, u32[]{:S(2)}) copy-start(f32[4,16,64]{2,1,0:T(8,128)} %param.10) | copy-start | bytes 49156
  0.0 2.9 %copy-start.2 = (bf16[1216,64]{0,1:T(8,128)(2,1)S(1)}, bf16[1216,64]{0,1:T(8,128)(2,1)}, u32[]{:S(2)}) copy-start(bf16[1216,64]{0,1:T(8,128)(2,1)} %param.17) | copy-start | bytes 466948
  0.0 2.9 %copy-start.1 = (bf16[64,1216]{1,0:T(8,128)(2,1)S(1)}, bf16[64,1216]{1,0:T(8,128)(2,1)}, u32[]{:S(2)}) copy-start(bf16[64,1216]{1,0:T(8,128)(2,1)} %w_in_ref.1) | copy-start | bytes 466948
  2.9 2.1 %copy-start = (bf16[1,1536,1216]{1,2,0:T(8,128)(2,1)S(1)}, bf16[1,1536,1216]{1,2,0:T(8,128)(2,1)}, u32[]{:S(2)}) copy-start(bf16[1,1536,1216]{1,2,0:T(8,128)(2,1)} %param.16) | copy-start | bytes 11206660

commit v3 on v2

v3 whole, which is shorter than its diff:
```python
import functools

import jax
import jax.numpy as jnp
from jax import lax
from jax.experimental import pallas as pl
from jax.experimental.pallas import tpu as pltpu
from jax.sharding import PartitionSpec as P

HEAD_DIM = 64
STEPS = 28
SHIFT_SIGMA = 3.0
EPS_NORM = 1e-06
MESH = pl.DeviceIdType.MESH
BF16 = jnp.bfloat16
F32 = jnp.float32


def sigma_at(position):
    level = 1.0 - position.astype(F32) / STEPS
    return SHIFT_SIGMA * level / (1.0 + (SHIFT_SIGMA - 1.0) * level)


def patch_of(index, micro_count, batch_rows):
    patch = jnp.zeros_like(index)
    for m in range(1, micro_count):
        patch = patch + jnp.where(index >= m * batch_rows, 1, 0)
    return patch


def kernel(
    dims,
    latent_ref, w_in_ref, mod_ref, gate_ref, kv_ref, w_final_ref, guide_ref, w_qkv_hbm, w_out_hbm,
    out_ref,
    w_qkv, w_out, xbuf, xfull, normed, keys, values, key_mask, head_mask, att_all, newx,
    speed, speeds, guided,
    w_sem, wo_sem, e_send, x_send, x_recv, a_send, a_recv, v_send, v_recv, g_send, g_recv,
):
    branches, sections, patches, groups, micro_count, batch_rows, img, txt, out_turned = dims
    b, s, p = lax.axis_index("cfg"), lax.axis_index("section"), lax.axis_index("patch")
    last = sections - 1
    _, rows, columns = newx.shape
    heads, old, _ = kv_ref.shape
    group_heads = heads // groups
    group_inner = group_heads * HEAD_DIM
    half = micro_count // branches

    def weight_copy(c, g):
        part = pl.ds(g * group_inner, group_inner)
        return pltpu.make_async_copy(w_qkv_hbm.at[c, part], w_qkv.at[c, part], w_sem.at[c, g])

    for g in range(groups):
        for c in range(3):
            weight_copy(c, g).start()
    out_copy = pltpu.make_async_copy(w_out_hbm, w_out, wo_sem)
    out_copy.start()

    others = [lax.rem(p + d, patches) for d in range(1, patches)]

    barrier = pltpu.get_barrier_semaphore()
    for q in others:
        pl.semaphore_signal(barrier, inc=1, device_id={"patch": q}, device_id_type=MESH)

    @pl.when(s > 0)
    def _():
        for q in range(patches):
            pl.semaphore_signal(
                barrier, inc=1, device_id={"section": s - 1, "patch": q}, device_id_type=MESH
            )

    @pl.when(s < last)
    def _():
        pl.semaphore_signal(barrier, inc=1, device_id={"section": last}, device_id_type=MESH)

    @pl.when(s == last)
    def _():
        for e in range(1, branches):
            for q in range(patches):
                pl.semaphore_signal(
                    barrier, inc=1, device_id={"cfg": lax.rem(b + e, branches), "patch": q},
                    device_id_type=MESH,
                )

    @pl.when(s < last)
    def _():
        pl.semaphore_wait(barrier, 2 * patches - 1)

    @pl.when(s == last)
    def _():
        pl.semaphore_wait(barrier, branches * patches - 1 + last)

    def x_copy(source, f, q, sems, target):
        return pltpu.make_async_remote_copy(
            src_ref=source.at[f], dst_ref=xbuf.at[f, p], send_sem=sems.at[f, q],
            recv_sem=x_recv.at[f, p], device_id=target, device_id_type=MESH,
        )

    def embed_copy(f, q):
        return pltpu.make_async_remote_copy(
            src_ref=xbuf.at[f, p], dst_ref=xbuf.at[f, p], send_sem=e_send.at[f, q],
            recv_sem=x_recv.at[f, p], device_id={"patch": q}, device_id_type=MESH,
        )

    def x_arrival(f, q):
        return pltpu.make_async_remote_copy(
            src_ref=newx.at[f], dst_ref=xbuf.at[f, q], send_sem=x_send.at[f, 0],
            recv_sem=x_recv.at[f, q], device_id={"patch": others[0]}, device_id_type=MESH,
        )

    @pl.when(s == 0)
    def _():
        embedded = jnp.dot(latent_ref[...], w_in_ref[...], preferred_element_type=F32)
        embedded = embedded.astype(BF16).reshape(micro_count, rows, columns)
        for f in range(micro_count):
            xbuf[f, p] = embedded[f]
            for q in others:
                embed_copy(f, q).start()

    key_index = lax.broadcasted_iota(jnp.int32, key_mask.shape, 0)
    key_mask[...] = jnp.where(key_index < img + txt, 1.0, 0.0)
    row_head = patch_of(lax.broadcasted_iota(jnp.int32, head_mask.shape, 0), group_heads, rows)
    feature = lax.broadcasted_iota(jnp.int32, head_mask.shape, 1)
    feature_head = patch_of(feature, group_heads, HEAD_DIM)
    head_mask[...] = jnp.where(row_head == feature_head, 1.0, 0.0)
    turned_mask = head_mask[...].T

    @pl.loop(0, groups)
    def _(g):
        for j in range(group_heads):
            own = slice(j * HEAD_DIM, (j + 1) * HEAD_DIM)
            pair = kv_ref[g * group_heads + j].astype(F32)
            key = pair[:, :HEAD_DIM]
            scale = lax.rsqrt(jnp.mean(key * key, axis=-1, keepdims=True) + EPS_NORM)
            keys[g, :, own] = (key * scale).astype(BF16)
            values[g, :, own] = pair[:, HEAD_DIM:].astype(BF16)

    def att_copy(f, g, q):
        return pltpu.make_async_remote_copy(
            src_ref=att_all.at[f, p, g], dst_ref=att_all.at[f, p, g], send_sem=a_send.at[f, q, g],
            recv_sem=a_recv.at[f, p, g], device_id={"patch": q}, device_id_type=MESH,
        )

    def att_arrival(f, g, q):
        return pltpu.make_async_remote_copy(
            src_ref=att_all.at[f, q, g], dst_ref=att_all.at[f, q, g], send_sem=a_send.at[f, q, g],
            recv_sem=a_recv.at[f, q, g], device_id={"patch": q}, device_id_type=MESH,
        )

    def out_part(f, q, g):
        start = pl.multiple_of(q * (groups * group_inner) + g * group_inner, group_inner)
        if out_turned:
            return lax.dot_general(
                att_all[f, q, g], w_out[:, pl.ds(start, group_inner)], (((1,), (1,)), ((), ())),
                preferred_element_type=F32,
            )
        return jnp.dot(
            att_all[f, q, g], w_out[pl.ds(start, group_inner)], preferred_element_type=F32
        )

    @pl.loop(0, micro_count)
    def _(f):
        for q in range(patches):

            @pl.when((s > 0) | (p != q))
            def _():
                x_arrival(f, q).wait_recv()

        for q in range(patches):
            xfull[:, q * columns : (q + 1) * columns] = xbuf[f, q].astype(F32)
        x = xfull[...]
        centred = x - jnp.mean(x, axis=-1, keepdims=True)
        var = jnp.mean(centred * centred, axis=-1, keepdims=True)
        unit = centred * lax.rsqrt(var + EPS_NORM)
        unit = (unit * (1.0 + mod_ref[1:2]) + mod_ref[0:1]).astype(BF16)
        for j in range(group_heads):
            normed[j * rows : (j + 1) * rows] = unit
        own_rows = pl.ds(pl.multiple_of(f * rows, rows), rows)

        for g in range(groups):
            part = slice(g * group_inner, (g + 1) * group_inner)

            @pl.when(f == 0)
            def _():
                for c in range(3):
                    weight_copy(c, g).wait()

            turned = []
            for c in range(2):
                product = lax.dot_general(
                    w_qkv[c, part], normed[...] if c == 0 else normed[:rows],
                    (((1,), (1,)), ((), ())), preferred_element_type=F32,
                )
                product = product.astype(BF16).astype(F32)
                product = product.reshape(group_heads, HEAD_DIM, product.shape[-1])
                scale = lax.rsqrt(jnp.mean(product * product, axis=1, keepdims=True) + EPS_NORM)
                turned.append((product * scale).astype(BF16).astype(F32))
            value = lax.dot_general(
                normed[:rows], w_qkv[2, part], (((1,), (1,)), ((), ())), preferred_element_type=F32
            )
            keys[g, own_rows] = turned[1].reshape(group_inner, rows).T.astype(BF16)
            values[g, own_rows] = value.astype(BF16)
            query = turned[0].reshape(turned_mask.shape) * (turned_mask * HEAD_DIM**-0.5)
            scores = jnp.dot(keys[g], query.astype(BF16), preferred_element_type=F32)
            power = jnp.exp(scores) * key_mask[...]
            share = 1.0 / jnp.sum(power, axis=0, keepdims=True)
            att = lax.dot_general(
                (power * share).astype(BF16), values[g], (((0,), (0,)), ((), ())),
                preferred_element_type=F32,
            )
            att = (att * head_mask[...]).reshape(group_heads, rows, group_inner)
            att_all[f, p, g] = jnp.sum(att, axis=0).astype(BF16)
            for q in others:
                att_copy(f, g, q).start()

        @pl.when(f == 0)
        def _():
            out_copy.wait()

        update = out_part(f, p, 0)
        for g in range(1, groups):
            update += out_part(f, p, g)
        for g in range(groups):
            for q in others:
                att_arrival(f, g, q).wait_recv()
                update += out_part(f, q, g)
        newx[f] = (xbuf[f, p].astype(F32) + gate_ref[...] * update).astype(BF16)

        @pl.when(s < last)
        def _():
            for q in range(patches):
                x_copy(newx, f, q, x_send, {"section": s + 1, "patch": q}).start()

    def v_copy(e, q):
        return pltpu.make_async_remote_copy(
            src_ref=speed.at[pl.ds(e * half, half), q], dst_ref=speeds.at[b, p],
            send_sem=v_send.at[e, q], recv_sem=v_recv.at[b, p],
            device_id={"cfg": e, "patch": q}, device_id_type=MESH,
        )

    def v_arrival(e, q):
        return pltpu.make_async_remote_copy(
            src_ref=speed.at[pl.ds(0, half), q], dst_ref=speeds.at[e, q],
            send_sem=v_send.at[e, q], recv_sem=v_recv.at[e, q],
            device_id={"cfg": e, "patch": q}, device_id_type=MESH,
        )

    def g_copy(t):
        return pltpu.make_async_remote_copy(
            src_ref=guided, dst_ref=guided, send_sem=g_send.at[t], recv_sem=g_recv,
            device_id={"section": t}, device_id_type=MESH,
        )

    @pl.when(s == last)
    def _():
        partial = lax.dot_general(
            newx[...].reshape(micro_count * rows, columns), w_final_ref[...], (((1,), (1,)), ((), ())), preferred_element_type=F32
        )
        speed[...] = partial.reshape(speed.shape)
        peers = []
        for e in range(branches):
            for d in range(patches):
                if e or d:
                    peers.append((lax.rem(b + e, branches), lax.rem(p + d, patches)))
        for e, q in peers:
            v_copy(e, q).start()
        speeds[b, p] = speed[pl.ds(b * half, half), p]
        for e, q in peers:
            v_arrival(e, q).wait_recv()
        conditional = jnp.sum(speeds[0], axis=0)
        unconditional = jnp.sum(speeds[1], axis=0)
        guided[...] = unconditional + guide_ref[0] * (conditional - unconditional)
        for t in range(last):
            g_copy(t).start()
        for e, q in peers:
            v_copy(e, q).wait_send()
        for t in range(last):
            g_copy(t).wait_send()

    @pl.loop(0, micro_count)
    def _(f):
        @pl.when(s == 0)
        def _():
            for q in others:
                embed_copy(f, q).wait_send()

        for g in range(groups):
            for q in others:
                att_copy(f, g, q).wait_send()

        @pl.when(s < last)
        def _():
            for q in range(patches):
                x_copy(newx, f, q, x_send, {"section": s + 1, "patch": q}).wait_send()

    @pl.when(s < last)
    def _():
        g_copy(s).wait_recv()

    out_ref[...] = guided[...]


def on_device(
    latent, w_in, modulation, w_qkv, text_kv, stale_kv, w_out, w_final, guidance, step_index
):
    branches, sections = lax.axis_size("cfg"), lax.axis_size("section")
    patches = lax.axis_size("patch")
    b, s, p = lax.axis_index("cfg"), lax.axis_index("section"), lax.axis_index("patch")
    micro_count, batch_rows, chan = latent.shape
    rows = micro_count * batch_rows
    own_rows = batch_rows // patches
    columns = w_in.shape[1]
    width = columns * patches
    local_inner = w_qkv.shape[2]
    heads = local_inner // HEAD_DIM
    inner = w_out.shape[1]
    txt, img = text_kv.shape[2], stale_kv.shape[2]
    old = -(-(txt + img) // 16) * 16
    half = micro_count // branches
    groups = next(g for g in (3, 2, 1) if g == 1 or local_inner % (g * 128) == 0)
    group_inner = local_inner // groups
    tall = heads // groups * batch_rows

    joined = jnp.concatenate([stale_kv[0, 0], text_kv[0, 0]], axis=0)
    joined = jnp.pad(joined, ((0, old - txt - img), (0, 0), (0, 0)))
    kv = jnp.transpose(joined, (1, 0, 2))
    mod = modulation[0, 0]
    gate = lax.dynamic_slice_in_dim(mod[2:3], p * columns, columns, 1)

    out_turned = group_inner % 128 == 0
    dims = (
        branches, sections, patches, groups, micro_count, batch_rows, img, txt, out_turned
    )
    vmem = pl.BlockSpec(memory_space=pltpu.VMEM)
    dma = pltpu.SemaphoreType.DMA
    guided = pl.pallas_call(
        functools.partial(kernel, dims),
        out_shape=jax.ShapeDtypeStruct((half, own_rows, chan), F32),
        in_specs=[vmem] * 6
        + [pl.BlockSpec(memory_space=pltpu.SMEM)]
        + [pl.BlockSpec(memory_space=pl.ANY)] * 2,
        out_specs=vmem,
        scratch_shapes=[
            pltpu.VMEM((3, local_inner, width), BF16),
            pltpu.VMEM((columns, inner) if out_turned else (inner, columns), BF16),
            pltpu.VMEM((micro_count, patches, batch_rows, columns), BF16),
            pltpu.VMEM((batch_rows, width), F32),
            pltpu.VMEM((tall, width), BF16),
            pltpu.VMEM((groups, old, group_inner), BF16),
            pltpu.VMEM((groups, old, group_inner), BF16),
            pltpu.VMEM((old, tall), F32),
            pltpu.VMEM((tall, group_inner), F32),
            pltpu.VMEM((micro_count, patches, groups, batch_rows, group_inner), BF16),
            pltpu.VMEM((micro_count, batch_rows, columns), BF16),
            pltpu.VMEM((micro_count, patches, own_rows, chan), F32),
            pltpu.VMEM((branches, patches, half, own_rows, chan), F32),
            pltpu.VMEM((half, own_rows, chan), F32),
            dma((3, groups)),
            dma,
            dma((micro_count, patches)),
            dma((micro_count, patches)),
            dma((micro_count, patches)),
            dma((micro_count, patches, groups)),
            dma((micro_count, patches, groups)),
            dma((branches, patches)),
            dma((branches, patches)),
            dma((sections,)),
            dma,
        ],
        compiler_params=pltpu.CompilerParams(
            collective_id=0, has_side_effects=True, vmem_limit_bytes=48 * 1024 * 1024
        ),
    )(
        latent.astype(BF16).reshape(rows, chan), w_in, mod, gate, kv, w_final.T, guidance,
        w_qkv[0], w_out[0].T if out_turned else w_out[0],
    )

    section_width = half * chan // sections
    flat_guided = jnp.transpose(guided, (1, 0, 2)).reshape(own_rows, half * chan)
    own_latent = lax.dynamic_slice(
        latent, (b * half, p * own_rows, 0), (half, own_rows, chan)
    )
    flat_latent = jnp.transpose(own_latent, (1, 0, 2)).reshape(own_rows, half * chan)
    step_size = sigma_at(step_index[0] + 1) - sigma_at(step_index[0])
    result = flat_latent + step_size * flat_guided
    return lax.dynamic_slice_in_dim(result, s * section_width, section_width, 1)


def solution(mesh):
    in_specs = (
        P(),
        P(None, "patch"),
        P("section", "cfg", None, None),
        P("section", None, "patch", None),
        P("section", "cfg", None, "patch", None),
        P("section", "cfg", None, "patch", None),
        P("section", None, "patch"),
        P("patch", None),
        P(),
        P(),
    )
    out_specs = P("patch", ("cfg", "section"))
    return jax.shard_map(
        on_device, mesh=mesh, in_specs=in_specs, out_specs=out_specs, check_vma=False
    )
```

time: 141 us -> 134 us (0.950)
  Pallas kernels: 134 us -> 127 us
    pallas_call x1, Pallas kernels: 134 us -> 127 us  [on_device(): pl.pallas_call(functools.partial(kernel, dims), out_shape=jax.ShapeDtypeS...]
where the time goes in v3:
time: 134 us
  Pallas kernels  127 us (95%)
  local copies, waits for them, and re-layouts  3.67 us (3%)
  between operations  1.48 us (1%)
  other arithmetic  1.35 us (1%)
    pallas_call x1, Pallas kernels, on_device(): pl.pallas_call(functools.partial(kernel, dims), out_shape=jax.ShapeDtypeS...  127 us

profile of v3, /device:TPU:0, one launch (start us, length us, event | category | flops | bytes accessed | tf_op | source)
XLA Modules:
  0.0 133.8 jit_solution(5582596065216674337)
XLA Ops:
  0.0 0.0 copy-start.3
  0.0 0.0 copy-start.4
  0.0 0.0 copy-start.2
  0.0 0.0 copy-start.1
  0.0 0.8 slice.4
  0.8 0.1 dynamic-slice_bitcast_fusion.gate_ref
  0.9 1.3 fusion.3.kv_ref
  2.2 0.0 copy-done.3
  2.2 0.0 copy-done.4
  2.9 0.0 copy-done.2
  2.9 0.0 copy-done.1
  2.9 0.0 copy-start
  2.9 2.0 %copy-done = bf16[1,1536,1216]{1,2,0:T(8,128)(2,1)S(1)} copy-done((bf16[1,1536,1216]{1,2,0:T(8,128)(2,1)S(1)}, bf16[1,1536,1216]{1,2,0:T(8,128)(2,1)}, u32[]{:S(2)}) %copy-start) | copy-done | bytes 3735576
  5.0 127.3 %shard_map.100 = f32[2,8,64]{2,1,0:T(8,128)S(1)} custom-call(bf16[64,64]{1,0:T(8,128)(2,1)S(1)} %bitcast.21, bf16[64,1216]{1,0:T(8,128)(2,1)S(1)} %copy-done.1, f32[3,2432]{1,0:T(4,128)S(1)} %bitcast.20, f32[1,1216]{1,0:T(1,128)S(1)} %dynamic-slice_bitcast_fusion.gate_ref, bf16[12,400,128]{2,1,0:T(8,128)(2,1)S(1)} %fusion.3.kv_ref, ...), custom_call_target="tpu_custom_call" | custom-call | tf_op jit(solution)/shard_map/pallas_call | solution.py:335
  133.1 0.1 add.41
  133.1 0.7 constant_dynamic-slice_fusion
  (4 shorter events, 0.0 us)
Async XLA Ops:
  0.0 2.2 %copy-start.3 = (f32[1,1,3,2432]{3,1,2,0:T(1,128)S(1)}, f32[1,1,3,2432]{3,1,2,0:T(1,128)}, u32[]{:S(2)}) copy-start(f32[1,1,3,2432]{3,1,2,0:T(1,128)} %param.12) | copy-start | bytes 87556
  0.0 2.2 %copy-start.4 = (f32[4,16,64]{2,1,0:T(8,128)S(1)}, f32[4,16,64]{2,1,0:T(8,128)}, u32[]{:S(2)}) copy-start(f32[4,16,64]{2,1,0:T(8,128)} %param.10) | copy-start | bytes 49156
  0.0 2.9 %copy-start.2 = (bf16[1216,64]{0,1:T(8,128)(2,1)S(1)}, bf16[1216,64]{0,1:T(8,128)(2,1)}, u32[]{:S(2)}) copy-start(bf16[1216,64]{0,1:T(8,128)(2,1)} %param.17) | copy-start | bytes 466948
  0.0 2.9 %copy-start.1 = (bf16[64,1216]{1,0:T(8,128)(2,1)S(1)}, bf16[64,1216]{1,0:T(8,128)(2,1)}, u32[]{:S(2)}) copy-start(bf16[64,1216]{1,0:T(8,128)(2,1)} %w_in_ref.1) | copy-start | bytes 466948
  2.9 2.1 %copy-start = (bf16[1,1536,1216]{1,2,0:T(8,128)(2,1)S(1)}, bf16[1,1536,1216]{1,2,0:T(8,128)(2,1)}, u32[]{:S(2)}) copy-start(bf16[1,1536,1216]{1,2,0:T(8,128)(2,1)} %param.16) | copy-start | bytes 11206660

commit v4 on v3

--- a/solution.py
+++ b/solution.py
@@ -30,17 +30,20 @@
 
 def kernel(
     dims,
-    latent_ref, w_in_ref, mod_ref, gate_ref, kv_ref, w_final_ref, guide_ref, w_qkv_hbm, w_out_hbm,
+    latent_ref, w_in_ref, mod_ref, text_ref, stale_ref, w_final_ref, guide_ref, w_qkv_hbm, w_out_hbm,
     out_ref,
-    w_qkv, w_out, xbuf, xfull, normed, keys, values, key_mask, head_mask, att_all, newx,
+    w_qkv, w_out, w_back, gate, xbuf, xfull, normed, keys, values, mask_old, mask_new, head_mask,
+    att_all, newx,
     speed, speeds, guided,
     w_sem, wo_sem, e_send, x_send, x_recv, a_send, a_recv, v_send, v_recv, g_send, g_recv,
 ):
     branches, sections, patches, groups, micro_count, batch_rows, img, txt, out_turned = dims
     b, s, p = lax.axis_index("cfg"), lax.axis_index("section"), lax.axis_index("patch")
     last = sections - 1
-    _, rows, columns = newx.shape
-    heads, old, _ = kv_ref.shape
+    phases, rows, columns = newx.shape
+    heads = text_ref.shape[0]
+    old, tall = mask_old.shape[1:]
+    per_phase = micro_count // phases
     group_heads = heads // groups
     group_inner = group_heads * HEAD_DIM
     half = micro_count // branches
@@ -110,29 +113,68 @@
     @pl.when(s == 0)
     def _():
         embedded = jnp.dot(latent_ref[...], w_in_ref[...], preferred_element_type=F32)
-        embedded = embedded.astype(BF16).reshape(micro_count, rows, columns)
-        for f in range(micro_count):
+        embedded = embedded.astype(BF16).reshape(phases, rows, columns)
+        for f in range(phases):
             xbuf[f, p] = embedded[f]
             for q in others:
                 embed_copy(f, q).start()
 
-    key_index = lax.broadcasted_iota(jnp.int32, key_mask.shape, 0)
-    key_mask[...] = jnp.where(key_index < img + txt, 1.0, 0.0)
+    def row_patch_of(column):
+        head = patch_of(column, group_heads, rows)
+        return patch_of(column - head * rows, per_phase, batch_rows)
+
+    key_index = lax.broadcasted_iota(jnp.int32, (old, tall), 0)
+    key_patch = patch_of(key_index, micro_count, batch_rows)
+    row_patch = row_patch_of(lax.broadcasted_iota(jnp.int32, (old, tall), 1))
+    is_text = (key_index >= img) & (key_index < img + txt)
+    for f in range(phases):
+        first = f * per_phase
+        seen = (key_patch < first) | (key_patch > row_patch + first)
+        mask_old[f] = jnp.where(is_text | ((key_index < img) & seen), 1.0, 0.0)
+    key_patch = patch_of(
+        lax.broadcasted_iota(jnp.int32, (rows, tall), 0), per_phase, batch_rows
+    )
+    row_patch = row_patch_of(lax.broadcasted_iota(jnp.int32, (rows, tall), 1))
+    mask_new[...] = jnp.where(key_patch <= row_patch, 1.0, 0.0)
     row_head = patch_of(lax.broadcasted_iota(jnp.int32, head_mask.shape, 0), group_heads, rows)
     feature = lax.broadcasted_iota(jnp.int32, head_mask.shape, 1)
     feature_head = patch_of(feature, group_heads, HEAD_DIM)
     head_mask[...] = jnp.where(row_head == feature_head, 1.0, 0.0)
     turned_mask = head_mask[...].T
 
+    for q in range(patches):
+
+        @pl.when(p == q)
+        def _():
+            gate[...] = mod_ref[2:3, q * columns : (q + 1) * columns]
+
     @pl.loop(0, groups)
     def _(g):
+        keys[g, img:] = jnp.zeros((old - img, group_inner), BF16)
+        values[g, img:] = jnp.zeros((old - img, group_inner), BF16)
         for j in range(group_heads):
             own = slice(j * HEAD_DIM, (j + 1) * HEAD_DIM)
-            pair = kv_ref[g * group_heads + j].astype(F32)
-            key = pair[:, :HEAD_DIM]
-            scale = lax.rsqrt(jnp.mean(key * key, axis=-1, keepdims=True) + EPS_NORM)
-            keys[g, :, own] = (key * scale).astype(BF16)
-            values[g, :, own] = pair[:, HEAD_DIM:].astype(BF16)
+            for source, start, count in ((stale_ref, 0, img), (text_ref, img, txt)):
+                pair = source[g * group_heads + j].astype(F32)
+                key = pair[:, :HEAD_DIM]
+                scale = lax.rsqrt(jnp.mean(key * key, axis=-1, keepdims=True) + EPS_NORM)
+                keys[g, start : start + count, own] = (key * scale).astype(BF16)
+                values[g, start : start + count, own] = pair[:, HEAD_DIM:].astype(BF16)
+
+    for g in range(groups):
+        for c in range(3):
+            weight_copy(c, g).wait()
+
+    def out_ready():
+        out_copy.wait()
+        if out_turned:
+            for g in range(patches * groups):
+                part = slice(g * group_inner, (g + 1) * group_inner)
+                w_back[part] = w_out[:, part].T
+
+    @pl.when(s > 0)
+    def _():
+        out_ready()
 
     def att_copy(f, g, q):
         return pltpu.make_async_remote_copy(
@@ -148,16 +190,12 @@
 
     def out_part(f, q, g):
         start = pl.multiple_of(q * (groups * group_inner) + g * group_inner, group_inner)
-        if out_turned:
-            return lax.dot_general(
-                att_all[f, q, g], w_out[:, pl.ds(start, group_inner)], (((1,), (1,)), ((), ())),
-                preferred_element_type=F32,
-            )
+        source = w_back if out_turned else w_out
         return jnp.dot(
-            att_all[f, q, g], w_out[pl.ds(start, group_inner)], preferred_element_type=F32
-        )
-
-    @pl.loop(0, micro_count)
+            att_all[f, q, g], source[pl.ds(start, group_inner)], preferred_element_type=F32
+        )
+
+    @pl.loop(0, phases)
     def _(f):
         for q in range(patches):
 
@@ -176,46 +214,62 @@
             normed[j * rows : (j + 1) * rows] = unit
         own_rows = pl.ds(pl.multiple_of(f * rows, rows), rows)
 
-        for g in range(groups):
+        def project(g):
             part = slice(g * group_inner, (g + 1) * group_inner)
-
-            @pl.when(f == 0)
-            def _():
-                for c in range(3):
-                    weight_copy(c, g).wait()
-
             turned = []
             for c in range(2):
                 product = lax.dot_general(
                     w_qkv[c, part], normed[...] if c == 0 else normed[:rows],
                     (((1,), (1,)), ((), ())), preferred_element_type=F32,
                 )
-                product = product.astype(BF16).astype(F32)
-                product = product.reshape(group_heads, HEAD_DIM, product.shape[-1])
-                scale = lax.rsqrt(jnp.mean(product * product, axis=1, keepdims=True) + EPS_NORM)
-                turned.append((product * scale).astype(BF16).astype(F32))
+                turned.append(product.astype(BF16))
             value = lax.dot_general(
                 normed[:rows], w_qkv[2, part], (((1,), (1,)), ((), ())), preferred_element_type=F32
             )
-            keys[g, own_rows] = turned[1].reshape(group_inner, rows).T.astype(BF16)
-            values[g, own_rows] = value.astype(BF16)
-            query = turned[0].reshape(turned_mask.shape) * (turned_mask * HEAD_DIM**-0.5)
-            scores = jnp.dot(keys[g], query.astype(BF16), preferred_element_type=F32)
-            power = jnp.exp(scores) * key_mask[...]
-            share = 1.0 / jnp.sum(power, axis=0, keepdims=True)
+            return turned[0], turned[1], value.astype(BF16)
+
+        def unit_heads(turned):
+            product = turned.astype(F32).reshape(group_heads, HEAD_DIM, turned.shape[-1])
+            scale = lax.rsqrt(jnp.mean(product * product, axis=1, keepdims=True) + EPS_NORM)
+            return (product * scale).astype(BF16).astype(F32).reshape(turned.shape)
+
+        def attend(g, query, key, value):
+            key = unit_heads(key).T.astype(BF16)
+            query = (unit_heads(query) * (turned_mask * HEAD_DIM**-0.5)).astype(BF16)
+            power_old = jnp.exp(jnp.dot(keys[g], query, preferred_element_type=F32)) * mask_old[f]
+            power_new = jnp.exp(jnp.dot(key, query, preferred_element_type=F32)) * mask_new[...]
+            total = jnp.sum(power_old, axis=0, keepdims=True) + jnp.sum(
+                power_new, axis=0, keepdims=True
+            )
+            share = 1.0 / total
             att = lax.dot_general(
-                (power * share).astype(BF16), values[g], (((0,), (0,)), ((), ())),
+                (power_old * share).astype(BF16), values[g], (((0,), (0,)), ((), ())),
+                preferred_element_type=F32,
+            )
+            att += lax.dot_general(
+                (power_new * share).astype(BF16), value, (((0,), (0,)), ((), ())),
                 preferred_element_type=F32,
             )
             att = (att * head_mask[...]).reshape(group_heads, rows, group_inner)
             att_all[f, p, g] = jnp.sum(att, axis=0).astype(BF16)
             for q in others:
                 att_copy(f, g, q).start()
-
-        @pl.when(f == 0)
+            return key, value
+
+        ahead = project(0)
+        fresh = []
+        for g in range(groups):
+            now = ahead
+            if g + 1 < groups:
+                ahead = project(g + 1)
+            fresh.append(attend(g, *now))
+
+        @pl.when((s == 0) & (f == 0))
         def _():
-            out_copy.wait()
-
+            out_ready()
+
+        for g in range(groups):
+            keys[g, own_rows], values[g, own_rows] = fresh[g]
         update = out_part(f, p, 0)
         for g in range(1, groups):
             update += out_part(f, p, g)
@@ -223,7 +277,7 @@
             for q in others:
                 att_arrival(f, g, q).wait_recv()
                 update += out_part(f, q, g)
-        newx[f] = (xbuf[f, p].astype(F32) + gate_ref[...] * update).astype(BF16)
+        newx[f] = (xbuf[f, p].astype(F32) + gate[...] * update).astype(BF16)
 
         @pl.when(s < last)
         def _():
@@ -253,7 +307,7 @@
     @pl.when(s == last)
     def _():
         partial = lax.dot_general(
-            newx[...].reshape(micro_count * rows, columns), w_final_ref[...], (((1,), (1,)), ((), ())), preferred_element_type=F32
+            newx[...].reshape(phases * rows, columns), w_final_ref[...], (((1,), (1,)), ((), ())), preferred_element_type=F32
         )
         speed[...] = partial.reshape(speed.shape)
         peers = []
@@ -276,7 +330,7 @@
         for t in range(last):
             g_copy(t).wait_send()
 
-    @pl.loop(0, micro_count)
+    @pl.loop(0, phases)
     def _(f):
         @pl.when(s == 0)
         def _():
@@ -318,14 +372,13 @@
     half = micro_count // branches
     groups = next(g for g in (3, 2, 1) if g == 1 or local_inner % (g * 128) == 0)
     group_inner = local_inner // groups
-    tall = heads // groups * batch_rows
-
-    joined = jnp.concatenate([stale_kv[0, 0], text_kv[0, 0]], axis=0)
-    joined = jnp.pad(joined, ((0, old - txt - img), (0, 0), (0, 0)))
-    kv = jnp.transpose(joined, (1, 0, 2))
-    mod = modulation[0, 0]
-    gate = lax.dynamic_slice_in_dim(mod[2:3], p * columns, columns, 1)
-
+    per_phase = 2 if micro_count % 2 == 0 else 1
+    phases = micro_count // per_phase
+    phase_rows = per_phase * batch_rows
+    tall = heads // groups * phase_rows
+
+    text = jnp.transpose(text_kv[0, 0], (1, 0, 2))
+    stale = jnp.transpose(stale_kv[0, 0], (1, 0, 2))
     out_turned = group_inner % 128 == 0
     dims = (
         branches, sections, patches, groups, micro_count, batch_rows, img, txt, out_turned
@@ -342,35 +395,39 @@
         scratch_shapes=[
             pltpu.VMEM((3, local_inner, width), BF16),
             pltpu.VMEM((columns, inner) if out_turned else (inner, columns), BF16),
-            pltpu.VMEM((micro_count, patches, batch_rows, columns), BF16),
-            pltpu.VMEM((batch_rows, width), F32),
+            pltpu.VMEM((inner, columns) if out_turned else (16, 128), BF16),
+            pltpu.VMEM((1, columns), F32),
+            pltpu.VMEM((phases, patches, phase_rows, columns), BF16),
+            pltpu.VMEM((phase_rows, width), F32),
             pltpu.VMEM((tall, width), BF16),
             pltpu.VMEM((groups, old, group_inner), BF16),
             pltpu.VMEM((groups, old, group_inner), BF16),
-            pltpu.VMEM((old, tall), F32),
+            pltpu.VMEM((phases, old, tall), F32),
+            pltpu.VMEM((phase_rows, tall), F32),
             pltpu.VMEM((tall, group_inner), F32),
-            pltpu.VMEM((micro_count, patches, groups, batch_rows, group_inner), BF16),
-            pltpu.VMEM((micro_count, batch_rows, columns), BF16),
+            pltpu.VMEM((phases, patches, groups, phase_rows, group_inner), BF16),
+            pltpu.VMEM((phases, phase_rows, columns), BF16),
             pltpu.VMEM((micro_count, patches, own_rows, chan), F32),
             pltpu.VMEM((branches, patches, half, own_rows, chan), F32),
             pltpu.VMEM((half, own_rows, chan), F32),
             dma((3, groups)),
             dma,
-            dma((micro_count, patches)),
-            dma((micro_count, patches)),
-            dma((micro_count, patches)),
-            dma((micro_count, patches, groups)),
-            dma((micro_count, patches, groups)),
+            dma((phases, patches)),
+            dma((phases, patches)),
+            dma((phases, patches)),
+            dma((phases, patches, groups)),
+            dma((phases, patches, groups)),
             dma((branches, patches)),
             dma((branches, patches)),
             dma((sections,)),
             dma,
         ],
         compiler_params=pltpu.CompilerParams(
-            collective_id=0, has_side_effects=True, vmem_limit_bytes=48 * 1024 * 1024
+            collective_id=0, has_side_effects=True, vmem_limit_bytes=60 * 1024 * 1024
         ),
     )(
-        latent.astype(BF16).reshape(rows, chan), w_in, mod, gate, kv, w_final.T, guidance,
+        latent.astype(BF16).reshape(rows, chan), w_in, modulation[0, 0], text, stale, w_final.T,
+        guidance,
         w_qkv[0], w_out[0].T if out_turned else w_out[0],
     )
 

time: 134 us -> 117 us (0.87)
  Pallas kernels: 127 us -> 111 us
  local copies, waits for them, and re-layouts: 3.67 us -> 2.12 us
    pallas_call x1, Pallas kernels: 127 us -> 111 us  [on_device(): pl.pallas_call(functools.partial(kernel, dims), out_shape=jax.ShapeDtypeS...]
    convert_element_type x1, other arithmetic: 0.01 us -> 1.36 us  [on_device(): latent.astype(BF16).reshape(rows, chan)]
where the time goes in v4:
time: 117 us
  Pallas kernels  111 us (95%)
  local copies, waits for them, and re-layouts  2.12 us (2%)
  other arithmetic  2.08 us (2%)
  between operations  1.41 us (1%)
    pallas_call x1, Pallas kernels, on_device(): pl.pallas_call(functools.partial(kernel, dims), out_shape=jax.ShapeDtypeS...  111 us

profile of v4, /device:TPU:0, one launch (start us, length us, event | category | flops | bytes accessed | tf_op | source)
XLA Modules:
  0.0 117.1 jit_solution(813898335715977735)
XLA Ops:
  0.0 1.4 %convert_element_type.13 = bf16[4,16,64]{2,1,0:T(8,128)(2,1)} convert(f32[4,16,64]{2,1,0:T(8,128)} %param.10) | non-fusion elementwise | flops 4096 | bytes 24576 | tf_op jit(solution)/shard_map/convert_element_type | solution.py:429
  1.4 1.4 %copy.14 = f32[1,1,3,2432]{3,2,1,0:T(4,128)} copy(f32[1,1,3,2432]{3,1,2,0:T(1,128)} %param.12) | data formatting | bytes 58368
  3.4 111.4 %shard_map.100 = f32[2,8,64]{2,1,0:T(8,128)} custom-call(bf16[64,64]{1,0:T(8,128)(2,1)} %bitcast.24, bf16[64,1216]{1,0:T(8,128)(2,1)} %w_in_ref.1, f32[3,2432]{1,0:T(4,128)} %bitcast.23, bf16[12,333,128]{2,1,0:T(8,128)(2,1)} %bitcast.20, bf16[12,64,128]{2,1,0:T(8,128)(2,1)} %bitcast.21, bf16[64,1216]{1,0:T(8,128)(2,1)} %bitcast.22, f32[1]{0:T(128)S(6)} %copy.15.guide_ref, ...), custom_call_target="tpu_custom_call" | custom-call | tf_op jit(solution)/shard_map/pallas_call | solution.py:388
  115.6 0.7 add_bitcast_fusion
  116.3 0.1 add.35
  116.4 0.7 constant_dynamic-slice_fusion
  (1 shorter events, 0.0 us)

commit v5 on v4

--- a/solution.py
+++ b/solution.py
@@ -112,7 +112,8 @@
 
     @pl.when(s == 0)
     def _():
-        embedded = jnp.dot(latent_ref[...], w_in_ref[...], preferred_element_type=F32)
+        start = latent_ref[...].astype(BF16).reshape(phases * rows, latent_ref.shape[2])
+        embedded = jnp.dot(start, w_in_ref[...], preferred_element_type=F32)
         embedded = embedded.astype(BF16).reshape(phases, rows, columns)
         for f in range(phases):
             xbuf[f, p] = embedded[f]
@@ -146,7 +147,7 @@
 
         @pl.when(p == q)
         def _():
-            gate[...] = mod_ref[2:3, q * columns : (q + 1) * columns]
+            gate[...] = mod_ref[2, :, q * columns : (q + 1) * columns]
 
     @pl.loop(0, groups)
     def _(g):
@@ -209,7 +210,7 @@
         centred = x - jnp.mean(x, axis=-1, keepdims=True)
         var = jnp.mean(centred * centred, axis=-1, keepdims=True)
         unit = centred * lax.rsqrt(var + EPS_NORM)
-        unit = (unit * (1.0 + mod_ref[1:2]) + mod_ref[0:1]).astype(BF16)
+        unit = (unit * (1.0 + mod_ref[1]) + mod_ref[0]).astype(BF16)
         for j in range(group_heads):
             normed[j * rows : (j + 1) * rows] = unit
         own_rows = pl.ds(pl.multiple_of(f * rows, rows), rows)
@@ -360,7 +361,6 @@
     patches = lax.axis_size("patch")
     b, s, p = lax.axis_index("cfg"), lax.axis_index("section"), lax.axis_index("patch")
     micro_count, batch_rows, chan = latent.shape
-    rows = micro_count * batch_rows
     own_rows = batch_rows // patches
     columns = w_in.shape[1]
     width = columns * patches
@@ -426,20 +426,25 @@
             collective_id=0, has_side_effects=True, vmem_limit_bytes=60 * 1024 * 1024
         ),
     )(
-        latent.astype(BF16).reshape(rows, chan), w_in, modulation[0, 0], text, stale, w_final.T,
+        latent, w_in, modulation.reshape(3, 1, width), text, stale, w_final.T,
         guidance,
         w_qkv[0], w_out[0].T if out_turned else w_out[0],
     )
 
     section_width = half * chan // sections
-    flat_guided = jnp.transpose(guided, (1, 0, 2)).reshape(own_rows, half * chan)
-    own_latent = lax.dynamic_slice(
-        latent, (b * half, p * own_rows, 0), (half, own_rows, chan)
-    )
-    flat_latent = jnp.transpose(own_latent, (1, 0, 2)).reshape(own_rows, half * chan)
     step_size = sigma_at(step_index[0] + 1) - sigma_at(step_index[0])
-    result = flat_latent + step_size * flat_guided
-    return lax.dynamic_slice_in_dim(result, s * section_width, section_width, 1)
+    if chan % section_width:
+        flat = jnp.transpose(guided, (1, 0, 2)).reshape(own_rows, half * chan)
+        own_latent = lax.dynamic_slice(
+            latent, (b * half, p * own_rows, 0), (half, own_rows, chan)
+        )
+        flat_latent = jnp.transpose(own_latent, (1, 0, 2)).reshape(own_rows, half * chan)
+        result = flat_latent + step_size * flat
+        return lax.dynamic_slice_in_dim(result, s * section_width, section_width, 1)
+    m, column = s * section_width // chan, s * section_width % chan
+    size = (1, own_rows, section_width)
+    own_latent = lax.dynamic_slice(latent, (b * half + m, p * own_rows, column), size)
+    return (own_latent + step_size * lax.dynamic_slice(guided, (m, 0, column), size))[0]
 
 
 def solution(mesh):

time: 117 us -> 114 us (0.974)
  local copies, waits for them, and re-layouts: 2.12 us -> 0 us
    squeeze x0 -> x1, other arithmetic: none -> 1.37 us  [on_device(): (own_latent + step_size * lax.dynamic_slice(guided, (m, 0, column), size)...]
    unnamed x1 -> x0, local copies, waits for them, and re-layouts: 1.37 us -> none
    convert_element_type x1 -> x0, other arithmetic: 1.36 us -> none  [on_device(): latent.astype(BF16).reshape(rows, chan)]
where the time goes in v5:
time: 114 us
  Pallas kernels  111 us (97%)
  between operations  1.4 us (1%)
  other arithmetic  1.37 us (1%)
    pallas_call x1, Pallas kernels, on_device(): pl.pallas_call(functools.partial(kernel, dims), out_shape=jax.ShapeDtypeS...  111 us

profile of v5, /device:TPU:0, one launch (start us, length us, event | category | flops | bytes accessed | tf_op | source)
XLA Modules:
  0.0 114.2 jit_solution(4205392249251819465)
XLA Ops:
  1.4 111.5 %shard_map.100 = f32[2,8,64]{2,1,0:T(8,128)} custom-call(f32[4,16,64]{2,1,0:T(8,128)} %latent_ref.1, bf16[64,1216]{1,0:T(8,128)(2,1)} %w_in_ref.1, f32[3,1,2432]{2,1,0:T(1,128)} %bitcast.20, bf16[12,333,128]{2,1,0:T(8,128)(2,1)} %bitcast.17, bf16[12,64,128]{2,1,0:T(8,128)(2,1)} %bitcast.18, bf16[64,1216]{1,0:T(8,128)(2,1)} %bitcast.19, ...), custom_call_target="tpu_custom_call" | custom-call | tf_op jit(solution)/shard_map/pallas_call | solution.py:388
  112.9 1.4 %add_bitcast_fusion = f32[8,16]{1,0:T(8,128)} fusion(f32[2,8,64]{2,1,0:T(8,128)} %shard_map.100, s32[]{:T(128)S(6)} %select_n.29, s32[]{:T(128)S(6)} %select_n.28, f32[4,16,64]{2,1,0:T(8,128)} %latent_ref.1, s32[]{:T(128)S(6)} %select_n.25, s32[]{:T(128)S(6)} %select_n.26, f32[]{:T(128)} %bitcast), kind=kLoop, calls=%fused_computation | loop fusion | flops 256 | bytes 1556 | tf_op jit(solution)/shard_map/squeeze | solution.py:447

commit v6 on v5

--- a/solution.py
+++ b/solution.py
@@ -282,7 +282,7 @@
 
         @pl.when(s < last)
         def _():
-            for q in range(patches):
+            for q in others + [p]:
                 x_copy(newx, f, q, x_send, {"section": s + 1, "patch": q}).start()
 
     def v_copy(e, q):

time: 114 us -> 114 us (level)
  no operation moved by 1% of the time
where the time goes in v6:
time: 114 us
  Pallas kernels  111 us (97%)
  between operations  1.4 us (1%)
  other arithmetic  1.37 us (1%)
    pallas_call x1, Pallas kernels, on_device(): pl.pallas_call(functools.partial(kernel, dims), out_shape=jax.ShapeDtypeS...  111 us

profile of v6, /device:TPU:0, one launch (start us, length us, event | category | flops | bytes accessed | tf_op | source)
XLA Modules:
  0.0 113.7 jit_solution(11714527731174704419)
XLA Ops:
  1.4 110.9 %shard_map.100 = f32[2,8,64]{2,1,0:T(8,128)} custom-call(f32[4,16,64]{2,1,0:T(8,128)} %latent_ref.1, bf16[64,1216]{1,0:T(8,128)(2,1)} %w_in_ref.1, f32[3,1,2432]{2,1,0:T(1,128)} %bitcast.20, bf16[12,333,128]{2,1,0:T(8,128)(2,1)} %bitcast.17, bf16[12,64,128]{2,1,0:T(8,128)(2,1)} %bitcast.18, bf16[64,1216]{1,0:T(8,128)(2,1)} %bitcast.19, ...), custom_call_target="tpu_custom_call" | custom-call | tf_op jit(solution)/shard_map/pallas_call | solution.py:388
  112.3 1.4 %add_bitcast_fusion = f32[8,16]{1,0:T(8,128)} fusion(f32[2,8,64]{2,1,0:T(8,128)} %shard_map.100, s32[]{:T(128)S(6)} %select_n.29, s32[]{:T(128)S(6)} %select_n.28, f32[4,16,64]{2,1,0:T(8,128)} %latent_ref.1, s32[]{:T(128)S(6)} %select_n.25, s32[]{:T(128)S(6)} %select_n.26, f32[]{:T(128)} %bitcast), kind=kLoop, calls=%fused_computation | loop fusion | flops 256 | bytes 1556 | tf_op jit(solution)/shard_map/squeeze | solution.py:447
